TPU v7x, 128 devices: a whole 4x4x4 slice. The times are simulated.
128 devices in a mesh: wide: 16 (over x_lo, z, core), narrow: 8 (over x_hi, y).
Axes of the slice: x: 4 (x_hi: 2, x_lo: 2; x = x_hi * 2 + x_lo), y: 4, z: 4, core: 2. Of those that a mesh axis runs over, the one named last changes fastest.
Arguments:
- residual: bfloat16 [1024, 4096], P(('wide', 'narrow')), may hold values from -6 to 6
- queries: bfloat16 [1024, 8192], P(('wide', 'narrow')), may hold values from -6 to 6
- key_cache: bfloat16 [1024, 256, 512], P(('wide', 'narrow')), may hold values from -6 to 6
- value_cache: bfloat16 [1024, 256, 512], P(('wide', 'narrow')), may hold values from -6 to 6
- new_keys: bfloat16 [1024, 512], P(('wide', 'narrow')), may hold values from -6 to 6
- new_values: bfloat16 [1024, 512], P(('wide', 'narrow')), may hold values from -6 to 6
- lengths: int32 [1024], P(('wide', 'narrow')), may hold values from 2 to 256, as said below
- out_weight: bfloat16 [8192, 4096], P('narrow'), may hold values from -0.25 to 0.25
- norm_gain: float32 [4096], replicated, may hold values from 0.25 to 1.75
- routes: int32 [1024, 8], P(('wide', 'narrow')), may hold values from 0 to 63, all different within a row; in each aligned block of 8 rows (0 to 7, 8 to 15, ...) at most 2 rows name the same one
- gate_probs: float32 [1024, 8], P(('wide', 'narrow')), may hold values from 0.02 to 1
- w_gate: bfloat16 [128, 4096, 384], P(('wide', 'narrow')), may hold values from -0.09375 to 0.09375
- w_up: bfloat16 [128, 4096, 384], P(('wide', 'narrow')), may hold values from -0.09375 to 0.09375
- w_down: bfloat16 [128, 384, 4096], P(('wide', 'narrow')), may hold values from -0.21875 to 0.21875
Outputs:
- mixed: bfloat16 [1024, 4096], P(('wide', 'narrow'))
Inputs may be any that keep to these rules, and one draw needn't show every extreme that they name: `lengths`: some request holds exactly 256 cached positions. `routes`: in the rows of one device (aligned blocks of 8 rows) no expert is named by more than 2 rows; some expert is named by exactly 2.
All inputs are finite; a program needn't handle non-finite values.
Results may differ from a plain program's by a relative error of at most 0.017.
Values may be sent and summed in bfloat16 or wider, within the bound.
A program may use at most 128 MiB of HBM per device.

v0:
```python
import jax
import jax.numpy as jnp
from jax import lax
from jax.sharding import PartitionSpec as P

D = 4096
HQ = 64
KVH = 4
HD = 128
TOP = 8
CACHE = 256


def attend_local(queries, cached_keys, cached_values, fresh_keys, fresh_values, length):
    batch_rows = queries.shape[0]
    scaling = HD ** (-0.5)
    grouped = queries.reshape(batch_rows, KVH, HQ // KVH, HD)
    key_heads = cached_keys.reshape(batch_rows, CACHE, KVH, HD)
    value_heads = cached_values.reshape(batch_rows, CACHE, KVH, HD)
    scores = (
        jnp.einsum("rgqd,rlgd->rgql", grouped, key_heads, preferred_element_type=jnp.float32)
        * scaling
    )
    own_score = (
        jnp.einsum(
            "rgqd,rgd->rgq",
            grouped,
            fresh_keys.reshape(batch_rows, KVH, HD),
            preferred_element_type=jnp.float32,
        )
        * scaling
    )
    visible = jnp.arange(CACHE, dtype=jnp.int32)[None, :] < length[:, None]
    scores = jnp.where(visible[:, None, None, :], scores, -jnp.inf)
    highest = jnp.maximum(jnp.max(scores, axis=-1), own_score)
    weights = jnp.exp(scores - highest[..., None])
    own_weight = jnp.exp(own_score - highest)
    normaliser = jnp.sum(weights, axis=-1) + own_weight
    weights = (weights / normaliser[..., None]).astype(jnp.bfloat16)
    own_weight = (own_weight / normaliser).astype(jnp.bfloat16)
    attended = jnp.einsum(
        "rgql,rlgd->rgqd", weights, value_heads, preferred_element_type=jnp.float32
    )
    attended = attended + own_weight.astype(jnp.float32)[..., None] * fresh_values.astype(
        jnp.float32
    ).reshape(batch_rows, KVH, 1, HD)
    return attended.reshape(batch_rows, HQ * HD).astype(jnp.bfloat16)


def expert_apply(token_rows, w_gate, w_up, w_down):
    gate_value = jnp.dot(token_rows, w_gate[0], preferred_element_type=jnp.float32)
    up_value = jnp.dot(token_rows, w_up[0], preferred_element_type=jnp.float32)
    active = (jax.nn.silu(gate_value) * up_value).astype(jnp.bfloat16)
    return jnp.dot(active, w_down[0], preferred_element_type=jnp.float32)


def local(
    residual,
    queries,
    key_cache,
    value_cache,
    new_keys,
    new_values,
    lengths,
    out_weight,
    norm_gain,
    routes,
    gate_probs,
    w_gate,
    w_up,
    w_down,
):
    request_rows = residual.shape[0]
    attended = attend_local(queries, key_cache, value_cache, new_keys, new_values, lengths)
    heads_local = lax.all_to_all(attended, "narrow", split_axis=1, concat_axis=0, tiled=True)
    attention_sum = lax.psum_scatter(
        jnp.dot(heads_local, out_weight, preferred_element_type=jnp.float32).astype(jnp.bfloat16),
        "narrow",
        scatter_dimension=0,
        tiled=True,
    ).astype(jnp.float32)
    stream = (residual.astype(jnp.float32) + attention_sum).astype(jnp.bfloat16)
    stream_float = stream.astype(jnp.float32)
    mean_square = jnp.mean(stream_float * stream_float, axis=-1, keepdims=True)
    normed = (stream_float * lax.rsqrt(mean_square + 1e-06) * norm_gain).astype(jnp.bfloat16)
    devices = lax.axis_size("wide") * lax.axis_size("narrow")
    experts = devices // 2
    capacity = 2 * ((request_rows * TOP + experts - 1) // experts)
    chosen = routes.reshape(-1)
    onehot = (chosen[:, None] == jnp.arange(experts, dtype=jnp.int32)[None, :]).astype(jnp.int32)
    earlier = jnp.cumsum(onehot, axis=0) - onehot
    slot_index = jnp.sum(onehot * earlier, axis=1)
    token_rows = jnp.repeat(normed, TOP, axis=0)
    target = chosen * capacity + slot_index
    packed = jnp.zeros((experts * capacity, D), jnp.bfloat16).at[target].set(token_rows)
    packed = jnp.broadcast_to(
        packed.reshape(experts, 1, capacity, D), (experts, 2, capacity, D)
    ).reshape(devices, capacity, D)
    arrived = lax.all_to_all(packed, ("wide", "narrow"), split_axis=0, concat_axis=0, tiled=True)
    part_sums = expert_apply(arrived.reshape(devices * capacity, D), w_gate, w_up, w_down).reshape(
        devices, capacity, D
    )
    returned = lax.all_to_all(
        part_sums.astype(jnp.bfloat16), ("wide", "narrow"), split_axis=0, concat_axis=0, tiled=True
    ).astype(part_sums.dtype)
    expert_out = (
        jnp.sum(returned.reshape(experts, 2, capacity, D), axis=1)
        .astype(jnp.bfloat16)
        .reshape(experts * capacity, D)
    )
    picked = expert_out[target].astype(jnp.float32).reshape(request_rows, TOP, D)
    shares = gate_probs / jnp.sum(gate_probs, axis=-1, keepdims=True)
    expert_mix = jnp.sum(shares[..., None] * picked, axis=1)
    return (stream_float + expert_mix).astype(jnp.bfloat16)


def solution(mesh):
    in_specs = (
        P(("wide", "narrow"), None),
        P(("wide", "narrow"), None),
        P(("wide", "narrow"), None, None),
        P(("wide", "narrow"), None, None),
        P(("wide", "narrow"), None),
        P(("wide", "narrow"), None),
        P(("wide", "narrow")),
        P("narrow", None),
        P(),
        P(("wide", "narrow"), None),
        P(("wide", "narrow"), None),
        P(("wide", "narrow"), None, None),
        P(("wide", "narrow"), None, None),
        P(("wide", "narrow"), None, None),
    )
    out_specs = P(("wide", "narrow"), None)
    return jax.shard_map(local, mesh=mesh, in_specs=in_specs, out_specs=out_specs, check_vma=False)
```

profile of v0, /device:TPU:1, one launch (start us, length us, event | category | flops | bytes accessed | tf_op | source)
XLA Modules:
  0.0 220.4 jit_solution(4039894279182183515)
XLA Ops:
  6.5 0.0 copy-start
  6.5 0.0 reduce-scatter.2.cloned.1.call-start
  6.5 0.9 iota_compare_fusion.1
  7.4 1.2 fusion.43
  8.7 2.4 %fusion.51 = (f32[8,4,16]{2,1,0:T(4,128)S(1)}, f32[8,4,16,256]{3,2,1,0:T(8,128)S(1)}) fusion(bf16[8,4,16,128]{3,0,2,1:T(8,128)(2,1)} %bitcast.74, pred[8,256]{1,0:T(8,128)(4,1)S(1)} %iota_compare_fusion.1, bf16[8,256,512]{2,1,0:T(8,128)(2,1)} %param.16), kind=kOutput, calls=%fused_computation.64 | convolution fusion | flops 33947136 | bytes 2756608 | tf_op jit(solution)/shard_map/rgqd,rlgd->rgql/dot_general | solution.py:21
  11.1 0.3 fusion.33
  11.4 0.0 copy-done.7
  11.5 0.0 copy-done.9
  11.5 0.5 fusion.26
  11.9 0.1 convert_element_type.67
  12.0 0.1 copy.30
  12.1 14.2 %all_to_all.26 = bf16[8,8,1024]{2,0,1:T(8,128)(2,1)S(1)} all-to-all(bf16[8,8,1024]{2,0,1:T(8,128)(2,1)S(1)} %copy.30), channel_id=1, replica_groups=mesh['wide'=16,'narrow'=8] {'narrow'}, dimensions={1} | all-to-all | bytes 262144 | tf_op jit(solution)/shard_map/all_to_all | solution.py:75
  26.3 5.8 %convolution_convert_fusion.1 = bf16[64,4096]{1,0:T(8,128)(2,1)} fusion(bf16[1024,4096]{1,0:T(8,128)(2,1)} %param.21, bf16[8,8,1024]{2,0,1:T(8,128)(2,1)S(1)} %all_to_all.26), kind=kOutput, calls=%fused_computation.3 | convolution fusion | flops 537133056 | bytes 9043968 | tf_op jit(solution)/shard_map/dot_general | solution.py:77
  32.1 0.0 reduce-scatter.2.cloned.1.call-update
  32.1 0.0 copy-done.5
  32.1 0.1 eq.15
  32.2 0.1 mul.95
  32.3 0.1 fusion.46
  32.4 0.1 reduce_window_sum.11
  32.5 0.2 select_reduce_fusion
  32.6 67.6 %reduce-scatter.2.cloned.1.call-done = bf16[8,4096]{1,0:T(8,128)(2,1)} async-done(((bf16[64,4096]{1,0:T(8,128)(2,1)}), bf16[8,4096]{1,0:T(8,128)(2,1)}) %reduce-scatter.2.cloned.1.call-update) | async-done | bytes 65552 | tf_op jit(solution)/shard_map/reduce_scatter | solution.py:76
  100.2 0.0 copy-done.2
  100.2 1.0 fusion.38
  101.2 0.0 copy-done.6
  101.2 0.9 fusion.40
  102.1 2.4 %scatter_custom_fusion = bf16[128,4096]{1,0:T(8,128)(2,1)} fusion(s32[64]{0:T(128)S(1)} %fusion.50, bf16[]{:T(256)} %constant.13.clone.1, bf16[8,4096]{1,0:T(8,128)(2,1)S(1)} %fusion.40), kind=kCustom, calls=%fused_computation.24 | custom fusion | bytes 1114114 | tf_op jit(solution)/shard_map/scatter | solution.py:95
  104.6 2.5 %broadcast_in_dim.24 = bf16[64,2,4096]{2,1,0:T(2,128)(2,1)} reshape(bf16[128,4096]{1,0:T(8,128)(2,1)} %scatter_custom_fusion) | data formatting | bytes 2097152 | tf_op jit(solution)/shard_map/broadcast_in_dim | solution.py:96
  107.1 3.7 %broadcast_in_dim.25 = bf16[64,2,2,4096]{3,2,1,0:T(2,128)(2,1)S(1)} broadcast(bf16[64,2,4096]{2,1,0:T(2,128)(2,1)} %broadcast_in_dim.24), dimensions={0,2,3} | broadcast | bytes 3145728 | tf_op jit(solution)/shard_map/broadcast_in_dim | solution.py:96
  110.8 37.6 %all_to_all.27 = bf16[128,2,4096]{2,1,0:T(2,128)(2,1)} all-to-all(bf16[128,2,4096]{2,1,0:T(2,128)(2,1)S(1)} %bitcast.72), channel_id=1, replica_groups=mesh['wide'=16,'narrow'=8] {'wide','narrow'}, dimensions={0} | all-to-all | bytes 4194304 | tf_op jit(solution)/shard_map/all_to_all | solution.py:99
  148.5 4.1 %reshape.113 = bf16[256,4096]{1,0:T(8,128)(2,1)} reshape(bf16[128,2,4096]{2,1,0:T(2,128)(2,1)} %all_to_all.27) | data formatting | bytes 4194304 | tf_op jit(solution)/shard_map/reshape | solution.py:100
  152.6 3.9 %fusion.3 = f32[256,384]{1,0:T(8,128)S(1)} fusion(bf16[256,4096]{1,0:T(8,128)(2,1)} %reshape.113, bf16[1,4096,384]{2,1,0:T(8,128)(2,1)} %param.25), kind=kOutput, calls=%fused_computation.7 | convolution fusion | flops 805306368 | bytes 5636096 | tf_op jit(solution)/shard_map/dot_general | solution.py:51
  156.5 0.0 copy-done.1
  156.5 0.1 copy-done.8
  156.7 1.9 fusion.20
  158.6 1.0 dot_general.29
  159.6 0.0 copy-done
  159.6 1.3 convolution_convert_fusion
  160.9 3.5 %copy.32 = bf16[128,2,4096]{2,1,0:T(2,128)(2,1)} copy(bf16[128,2,4096]{2,0,1:T(8,128)(2,1)S(1)} %convolution_convert_fusion) | data formatting | bytes 4194304 | tf_op jit(solution)/shard_map/convert_element_type | solution.py:104
  164.4 6.7 %all-to-all-start.2 = ((bf16[128,2,4096]{2,1,0:T(2,128)(2,1)}), bf16[128,2,4096]{2,1,0:T(2,128)(2,1)}, u32[]{:S(2)}, u32[]{:S(2)}) async-start(bf16[128,2,4096]{2,1,0:T(2,128)(2,1)} %copy.32), calls=%async_computation.3 | async-start | bytes 4194304 | tf_op jit(solution)/shard_map/all_to_all | solution.py:103
  171.1 0.1 reduce_sum.57
  171.2 0.1 broadcast_divide_fusion
  171.3 27.9 %all-to-all-done.2 = bf16[128,2,4096]{2,1,0:T(2,128)(2,1)} async-done(((bf16[128,2,4096]{2,1,0:T(2,128)(2,1)}), bf16[128,2,4096]{2,1,0:T(2,128)(2,1)}, u32[]{:S(2)}, u32[]{:S(2)}) %all-to-all-start.2) | async-done | bytes 2097184 | tf_op jit(solution)/shard_map/all_to_all | solution.py:103
  199.3 6.3 %bitcast_reduce_fusion = bf16[64,2,4096]{2,1,0:T(2,128)(2,1)} fusion(bf16[128,2,4096]{2,1,0:T(2,128)(2,1)} %all-to-all-done.2), kind=kLoop, calls=%fused_computation.15 | loop fusion | flops 524288 | bytes 3145728 | tf_op jit(solution)/shard_map/reduce_sum | solution.py:107
  205.5 2.3 %convert_element_type.77 = bf16[128,4096]{1,0:T(8,128)(2,1)} reshape(bf16[64,2,4096]{2,1,0:T(2,128)(2,1)} %bitcast_reduce_fusion) | data formatting | bytes 2097152 | tf_op jit(solution)/shard_map/convert_element_type | solution.py:108
  207.8 3.6 %gather_fusion = bf16[64,4096]{1,0:T(8,128)(2,1)} fusion(bf16[128,4096]{1,0:T(8,128)(2,1)} %convert_element_type.77, s32[1024]{0:T(1024)S(1)} %pad_clamp_fusion), kind=kCustom, calls=%fused_computation | custom fusion | bytes 1048832 | tf_op jit(solution)/shard_map/gather | solution.py:111
  211.4 1.5 fusion.29
  212.9 0.0 copy-done.3
  212.9 0.7 fusion.41
  (18 shorter events, 0.1 us)
Async XLA Ops:
  6.5 153.1 %copy-start = (bf16[1,384,4096]{2,1,0:T(8,128)(2,1)S(1)}, bf16[1,384,4096]{2,1,0:T(8,128)(2,1)}, u32[]{:S(2)}) copy-start(bf16[1,384,4096]{2,1,0:T(8,128)(2,1)} %param.27) | copy-start | bytes 9437188
  6.5 4.9 %copy-start.7 = (bf16[8,512]{1,0:T(8,128)(2,1)S(1)}, bf16[8,512]{1,0:T(8,128)(2,1)}, u32[]{:S(2)}) copy-start(bf16[8,512]{1,0:T(8,128)(2,1)} %param.19) | copy-start | bytes 24580
  6.5 93.7 %reduce-scatter.2.cloned.1.call-start = ((), (), s32[]{:S(2)}) async-start(), calls=%async_computation.4 | async-start | bytes 589824 | tf_op jit(solution)/shard_map/reduce_scatter | solution.py:76
  6.5 4.9 %copy-start.9 = (bf16[8,256,512]{2,1,0:T(8,128)(2,1)S(1)}, bf16[8,256,512]{2,1,0:T(8,128)(2,1)}, u32[]{:S(2)}) copy-start(bf16[8,256,512]{2,1,0:T(8,128)(2,1)} %param.17) | copy-start | bytes 6291460
  26.3 5.8 %copy-start.5 = (s32[8,8]{1,0:T(8,128)S(1)}, s32[8,8]{1,0:T(8,128)}, u32[]{:S(2)}) copy-start(s32[8,8]{1,0:T(8,128)} %param.23) | copy-start | bytes 772
  26.3 73.9 %copy-start.2 = (bf16[8,4096]{1,0:T(8,128)(2,1)S(1)}, bf16[8,4096]{1,0:T(8,128)(2,1)}, u32[]{:S(2)}) copy-start(bf16[8,4096]{1,0:T(8,128)(2,1)} %param.14) | copy-start | bytes 196612
  26.3 74.9 %copy-start.6 = (f32[4096]{0:T(1024)S(1)}, f32[4096]{0:T(1024)}, u32[]{:S(2)}) copy-start(f32[4096]{0:T(1024)} %param.22) | copy-start | bytes 49156
  152.6 4.0 %copy-start.1 = (bf16[256,4096]{1,0:T(8,128)(2,1)S(1)}, bf16[256,4096]{1,0:T(8,128)(2,1)}, u32[]{:S(2)}) copy-start(bf16[256,4096]{1,0:T(8,128)(2,1)} %reshape.113) | copy-start | bytes 6291460
  152.6 4.1 %copy-start.8 = (bf16[1,4096,384]{2,1,0:T(8,128)(2,1)S(1)}, bf16[1,4096,384]{2,1,0:T(8,128)(2,1)}, u32[]{:S(2)}) copy-start(bf16[1,4096,384]{2,1,0:T(8,128)(2,1)} %param.26) | copy-start | bytes 9437188
  164.4 6.8 %copy-start.4 = (f32[8,8]{1,0:T(8,128)S(1)}, f32[8,8]{1,0:T(8,128)}, u32[]{:S(2)}) copy-start(f32[8,8]{1,0:T(8,128)} %param.24) | copy-start | bytes 772
  164.4 34.9 %all-to-all-start.2 = ((bf16[128,2,4096]{2,1,0:T(2,128)(2,1)}), bf16[128,2,4096]{2,1,0:T(2,128)(2,1)}, u32[]{:S(2)}, u32[]{:S(2)}) async-start(bf16[128,2,4096]{2,1,0:T(2,128)(2,1)} %copy.32), calls=%async_computation.3 | async-start | bytes 4194304 | tf_op jit(solution)/shard_map/all_to_all | solution.py:103
  207.8 5.1 %copy-start.3 = (bf16[8,4096]{1,0:T(8,128)(2,1)S(1)}, bf16[8,4096]{1,0:T(8,128)(2,1)}, u32[]{:S(2)}) copy-start(bf16[8,4096]{1,0:T(8,128)(2,1)} %reduce-scatter.2.cloned.1.call-done) | copy-start | bytes 196612
Sparse Core Ops, SparseCore 0:
  32.2 67.9 reduce-scatter.1
where the time goes:
time: 221 us; the launch traced here: 220 us
  waiting for transfers between devices  95.5 us (43%)
  blocking collectives  51.9 us (23%)
  local copies, waits for them, and re-layouts  23.6 us (11%)
  matrix products  17 us (8%)
  between operations  13.6 us (6%)
  other arithmetic  12.1 us (5%)
  starting transfers between devices  6.74 us (3%)
    reduce_scatter x1, waiting for transfers between devices, local(): lax.psum_scatter(jnp.dot(heads_local, out_weight, preferred_element_type=...  67.6 us
    all_to_all x1, blocking collectives, local(): lax.all_to_all(packed, ('wide', 'narrow'), split_axis=0, concat_axis=0, t...  37.6 us
    all_to_all x1, waiting for transfers between devices, local(): lax.all_to_all(part_sums.astype(jnp.bfloat16), ('wide', 'narrow'), split_...  27.9 us
    all_to_all x1, blocking collectives, local(): lax.all_to_all(attended, 'narrow', split_axis=1, concat_axis=0, tiled=True)  14.2 us
    all_to_all x1, starting transfers between devices, local(): lax.all_to_all(part_sums.astype(jnp.bfloat16), ('wide', 'narrow'), split_...  6.74 us
    reduce_sum x1, other arithmetic, local(): jnp.sum(returned.reshape(experts, 2, capacity, D), axis=1)  6.26 us
    broadcast_in_dim x2, local copies, waits for them, and re-layouts, local(): jnp.broadcast_to(packed.reshape(experts, 1, capacity, D), (experts, 2, ca...  6.25 us
    dot_general x1, matrix products, local(): jnp.dot(heads_local, out_weight, preferred_element_type=jnp.float32)  5.78 us
  transfers between devices with their start and end apart: 2, of which 2 were waited for; matrix products, arithmetic and copies ran while one was open for 0% of the time, Pallas kernels for 0%

commit v1 on v0

v1 whole, which is shorter than its diff:
```python
import functools

import jax
import jax.numpy as jnp
from jax import lax
from jax.experimental import pallas as pl
from jax.experimental.pallas import tpu as pltpu
from jax.sharding import PartitionSpec as P

MESH = pl.DeviceIdType.MESH
F32 = jnp.float32
BF16 = jnp.bfloat16

D = 4096
HALF = 2048
HQ = 64
KVH = 4
HD = 128
TOP = 8
CACHE = 256
ROWS = 8
EH = 384

CW = (640, 640, 768)
OFF = (0, 640, 1280)
ORD = ((0, 1, 2), (1, 2, 0), (2, 0, 1))
STEPS = (1, 3, 2)


def coords():
    w, n = lax.axis_index("wide"), lax.axis_index("narrow")
    c = lax.rem(w, 2)
    z = lax.rem(lax.div(w, 2), 4)
    x = lax.div(n, 4) * 2 + lax.div(w, 8)
    return (x, lax.rem(n, 4), z), c, w * 8 + n, n


def device(pos, c):
    x, y, z = pos
    return (lax.rem(x, 2) * 8 + z * 2 + c, lax.div(x, 2) * 4 + y)


def shift(pos, axis, d):
    moved = list(pos)
    moved[axis] = lax.rem(moved[axis] + d, 4)
    return tuple(moved)


def remote(src, dst, ssem, rsem, target):
    return pltpu.make_async_remote_copy(
        src_ref=src, dst_ref=dst, send_sem=ssem, recv_sem=rsem, device_id=target, device_id_type=MESH
    )


def line_index(pos, p, stage, q, half=None):
    order = ORD[p]
    idx = list(pos)
    idx[order[stage]] = q
    for s in range(stage):
        idx[order[s]] = slice(None)
    if half is not None:
        idx[order[0]] = pl.ds(2 * half, 2)
    return tuple(idx)


def slab_index(p, first=slice(None), second=slice(None)):
    order = ORD[p]
    spec = {order[0]: first, order[1]: second}
    return tuple(spec[axis] for axis in range(3) if axis != order[2])


def kernel(
    residual, queries, key_cache, value_cache, new_keys, new_values, lengths, out_weight, norm_gain,
    routes, gate_probs, w_gate, w_up, w_down,
    out,
    keys, values, wo, wgu, wd, att, att_rx, a_mat, y_tx, y_rx, res_tx, res_rx, sq_tx, sq_rx,
    share, gh0, gh1, gh2, acc, act, p0, p1, p2, ra0, ra1, ra2, rx0, rx1, rx2, ry0, ry1, ry2,
    rz0, rz1, rz2, kept, fin_tx, fin_rx,
    lsem, pair_s, pair_r, a2a_s, a2a_r, af_s, af_r, y_s, y_r, sh_s, sh_r,
    g1_s, g1_r, g3_s, g3_r, d_s, d_r, act_s, act_r, q3_s, q3_r, q1_s, q1_r,
):
    pos, c, me, n_me = coords()
    x, y, z = pos
    sib = device(pos, 1 - c)
    gh = (gh0, gh1, gh2)
    part = (p0, p1, p2)
    ra, rx, ry, rz = (ra0, ra1, ra2), (rx0, rx1, rx2), (ry0, ry1, ry2), (rz0, rz1, rz2)
    own_cols = pl.ds(pl.multiple_of(c * HALF, HALF), HALF)
    other_cols = pl.ds(pl.multiple_of((1 - c) * HALF, HALF), HALF)
    sends = []

    def send(src, dst, ssem, rsem, target, keep=True):
        copy = remote(src, dst, ssem, rsem, target)
        copy.start()
        if keep:
            sends.append(copy)

    def arrived(dst, ssem, rsem):
        remote(dst, dst, ssem, rsem, sib).wait_recv()

    group = [(dx, dy) for dx in range(2) for dy in range(4)]

    def member(dx, dy):
        gx = x if dx == 0 else 3 - x
        gy = lax.rem(y + dy, 4)
        return (gx, gy, z), lax.div(gx, 2) * 4 + gy

    local = [
        pltpu.make_async_copy(key_cache, keys, lsem.at[0]),
        pltpu.make_async_copy(value_cache, values, lsem.at[1]),
        pltpu.make_async_copy(out_weight.at[:, own_cols], wo, lsem.at[2]),
        pltpu.make_async_copy(w_gate.at[0], wgu.at[:, pl.ds(0, EH)], lsem.at[3]),
        pltpu.make_async_copy(w_up.at[0], wgu.at[:, pl.ds(EH, EH)], lsem.at[4]),
        pltpu.make_async_copy(w_down.at[0, :, own_cols], wd.at[c], lsem.at[5]),
    ]
    for copy in local[:3]:
        copy.start()

    barrier = pltpu.get_barrier_semaphore()
    partners = [sib] + [device(shift(pos, a, d), c) for a in range(3) for d in STEPS]
    partners += [device(member(1, dy)[0], c) for dy in (1, 2, 3)]
    for partner in partners:
        pl.semaphore_signal(barrier, inc=1, device_id=partner, device_id_type=MESH)

    probs = gate_probs[...]
    shares = probs / jnp.sum(probs, axis=-1, keepdims=True)
    lanes = lax.broadcasted_iota(jnp.int32, (ROWS, 128), 1)
    dense = jnp.zeros((ROWS, 128), F32)
    chosen = routes[...]
    for k in range(TOP):
        dense = dense + jnp.where(chosen[:, k : k + 1] == lanes, shares[:, k : k + 1], 0.0)
    share[x, y, z, c] = dense
    res_tx[...] = residual[:, other_cols].astype(F32)

    pl.semaphore_wait(barrier, len(partners))
    send(res_tx, res_rx, pair_s.at[0], pair_r.at[0], sib)
    for k, d in enumerate(STEPS):
        view = share.at[x, y, z, c]
        send(view, view, sh_s.at[0, k], sh_r.at[0, k], device(shift(pos, 0, d), c))

    local[0].wait()
    local[1].wait()
    for copy in local[3:]:
        copy.start()
    send(w_down.at[0, :, other_cols], wd.at[c], pair_s.at[1], pair_r.at[1], sib)
    scaling = HD ** (-0.5)
    row_request = lax.rem(lax.broadcasted_iota(jnp.int32, (128, CACHE), 0), ROWS)
    limit = jnp.zeros((128, CACHE), jnp.int32)
    for r in range(ROWS):
        limit = jnp.where(row_request == r, lengths[r], limit)
    visible = lax.broadcasted_iota(jnp.int32, (128, CACHE), 1) < limit
    for g in range(KVH):
        cols = slice(g * HD, (g + 1) * HD)
        q = jnp.concatenate(
            [queries[:, (g * 16 + h) * HD : (g * 16 + h + 1) * HD].astype(F32) for h in range(16)], axis=0
        )
        scores = lax.dot_general(
            q.astype(BF16), keys[:, :, cols].reshape(ROWS * CACHE, HD), (((1,), (1,)), ((), ())),
            preferred_element_type=F32,
        )
        picked = scores[:, :CACHE]
        for r in range(1, ROWS):
            picked = jnp.where(row_request == r, scores[:, r * CACHE : (r + 1) * CACHE], picked)
        picked = jnp.where(visible, picked * scaling, -jnp.inf)
        fresh = jnp.concatenate([new_keys[:, cols].astype(F32)] * 16, axis=0)
        own = jnp.sum(q * fresh, axis=-1, keepdims=True) * scaling
        highest = jnp.maximum(jnp.max(picked, axis=-1, keepdims=True), own)
        weights = jnp.exp(picked - highest)
        own = jnp.exp(own - highest)
        norm = jnp.sum(weights, axis=-1, keepdims=True) + own
        weights = weights / norm
        own = (own / norm).astype(BF16).astype(F32)
        spread = jnp.concatenate(
            [jnp.where(row_request == r, weights, 0.0).astype(BF16) for r in range(ROWS)], axis=1
        )
        got = jnp.dot(spread, values[:, :, cols].reshape(ROWS * CACHE, HD), preferred_element_type=F32)
        got = got + own * jnp.concatenate([new_values[:, cols].astype(F32)] * 16, axis=0)
        att[2 * g : 2 * g + 2] = got.astype(BF16).reshape(2, 64, HD)

    mine = pltpu.make_async_copy(att.at[n_me], att_rx.at[n_me, c], lsem.at[6])
    mine.start()
    for i, (dx, dy) in enumerate(group):
        if i:
            target, n = member(dx, dy)
            send(att.at[n], att_rx.at[n_me, c], a2a_s.at[i], a2a_r.at[i], device(target, c))
    for k, d in enumerate(STEPS):
        view = share.at[lax.rem(x + 4 - d, 4), y, z, c]
        arrived(view, sh_s.at[0, k], sh_r.at[0, k])
    for k, d in enumerate(STEPS):
        view = share.at[:, y, z, c]
        send(view, view, sh_s.at[1, k], sh_r.at[1, k], device(shift(pos, 1, d), c))
    mine.wait()
    for i, (dx, dy) in enumerate(group):
        _, n = member(dx, (4 - dy) % 4)
        view = att_rx.at[n, c]
        if i:
            arrived(view, a2a_s.at[i], a2a_r.at[i])
        send(view, view, af_s.at[i], af_r.at[i], sib)
    for i, (dx, dy) in enumerate(group):
        _, n = member(dx, (4 - dy) % 4)
        arrived(att_rx.at[n, 1 - c], af_s.at[i], af_r.at[i])

    heads = att_rx[...].astype(F32).reshape(16, 64, HD)
    for h in range(8):
        a_mat[:, h * HD : (h + 1) * HD] = heads[:, h * 8 : (h + 1) * 8].reshape(128, HD).astype(BF16)

    local[2].wait()
    for j in range(4):
        cols = pl.ds(j * 512, 512)
        sums = jnp.dot(a_mat[...], wo[:, cols], preferred_element_type=F32)
        y_tx[:, :, cols] = sums.astype(BF16).reshape(8, 16, 512)
        for i, (dx, dy) in enumerate(group):
            if i:
                target, n = member(dx, dy)
                send(y_tx.at[n, :, cols], y_rx.at[i, :, cols], y_s.at[j, i], y_r.at[j, i], device(target, c))
    for k, d in enumerate(STEPS):
        view = share.at[:, lax.rem(y + 4 - d, 4), z, c]
        arrived(view, sh_s.at[1, k], sh_r.at[1, k])
    for k, d in enumerate(STEPS):
        view = share.at[:, :, z, c]
        send(view, view, sh_s.at[2, k], sh_r.at[2, k], device(shift(pos, 2, d), c))
    acc[...] = jnp.zeros_like(acc)
    arrived(res_rx, pair_s.at[0], pair_r.at[0])
    own_res, other_res = residual[:, own_cols].astype(F32), res_rx[...]
    first = c == 0
    total = jnp.concatenate(
        [jnp.where(first, own_res, other_res), jnp.where(first, other_res, own_res)], axis=0
    )
    attention = y_tx[n_me].astype(F32)
    for i in range(1, 8):
        for j in range(4):
            arrived(y_rx.at[i, :, pl.ds(j * 512, 512)], y_s.at[j, i], y_r.at[j, i])
        attention = attention + y_rx[i].astype(F32)
    stream = (total + attention).astype(BF16).astype(F32)
    squares = jnp.sum(stream * stream, axis=-1, keepdims=True)
    sq_tx[...] = jnp.broadcast_to(squares, (16, 128))
    send(sq_tx, sq_rx, pair_s.at[2], pair_r.at[2], sib)
    kept[...] = stream
    arrived(sq_rx, pair_s.at[2], pair_r.at[2])
    mean = (squares + sq_rx[:, 0:1]) * (1.0 / D)
    normed = (stream * lax.rsqrt(mean + 1e-06) * norm_gain[:, own_cols]).astype(BF16)
    for p in range(3):
        gh[p][(c,) + pos] = normed[:, OFF[p] : OFF[p] + CW[p]]

    def block(p, idx):
        return gh[p].at[(c,) + idx]

    for p in range(3):
        a = ORD[p][0]
        for k, d in enumerate(STEPS):
            view = block(p, pos)
            send(view, view, g1_s.at[p, 0, k], g1_r.at[p, 0, k], device(shift(pos, a, d), c))

    def chunk(p, rel, q):
        order = ORD[p]
        idx = list(line_index(pos, p, 2, q))
        idx[order[1]] = lax.rem(pos[order[1]] + rel, 4)
        return idx

    def send_chunk(p, rel):
        a = ORD[p][2]
        view = block(p, tuple(chunk(p, rel, pos[a])))
        send(view, view, g3_s.at[p, rel, 0], g3_r.at[p, rel, 0], device(shift(pos, a, 1), c))
        send(view, view, g3_s.at[p, rel, 1], g3_r.at[p, rel, 1], device(shift(pos, a, 3), c))

    def half_chunk(p, rel, q, half):
        idx = chunk(p, rel, q)
        idx[ORD[p][0]] = pl.ds(2 * half, 2)
        return block(p, tuple(idx))

    for p in range(3):
        a, b = ORD[p][0], ORD[p][1]
        for k, d in enumerate(STEPS):
            view = block(p, line_index(pos, p, 0, lax.rem(pos[a] + 4 - d, 4)))
            arrived(view, g1_s.at[p, 0, k], g1_r.at[p, 0, k])
        view = block(p, line_index(pos, p, 1, pos[b]))
        for k, d in enumerate(STEPS):
            send(view, view, g1_s.at[p, 1, k], g1_r.at[p, 1, k], device(shift(pos, b, d), c))
        send_chunk(p, 0)
    for k, d in enumerate(STEPS):
        for p in range(3):
            b = ORD[p][1]
            view = block(p, line_index(pos, p, 1, lax.rem(pos[b] + 4 - d, 4)))
            arrived(view, g1_s.at[p, 1, k], g1_r.at[p, 1, k])
            send_chunk(p, 4 - d)

    def pass_on(rel):
        for p in range(3):
            a = ORD[p][2]
            left, right = lax.rem(pos[a] + 3, 4), lax.rem(pos[a] + 1, 4)
            arrived(block(p, tuple(chunk(p, rel, left))), g3_s.at[p, rel, 0], g3_r.at[p, rel, 0])
            view = half_chunk(p, rel, left, 0)
            send(view, view, g3_s.at[p, rel, 2], g3_r.at[p, rel, 2], device(shift(pos, a, 1), c), False)
            arrived(block(p, tuple(chunk(p, rel, right))), g3_s.at[p, rel, 1], g3_r.at[p, rel, 1])
            view = half_chunk(p, rel, right, 1)
            send(view, view, g3_s.at[p, rel, 3], g3_r.at[p, rel, 3], device(shift(pos, a, 3), c), False)

    def slab(p, d):
        a = ORD[p][2]
        return line_index(pos, p, 2, lax.rem(pos[a] + d, 4))

    def to_sibling(d):
        for p in range(3):
            view = block(p, slab(p, d))
            send(view, view, d_s.at[p, d], d_r.at[p, d], sib, False)

    for copy in local[3:]:
        copy.wait()
    to_sibling(0)

    @pl.loop(0, 8)
    def _(i):
        @pl.when(i == 1)
        def _():
            pass_on(0)

        @pl.when(i == 2)
        def _():
            for rel in (3, 1, 2):
                pass_on(rel)
            to_sibling(3)
            to_sibling(1)

        @pl.when(i == 6)
        def _():
            for rel in (0, 3, 1, 2):
                for p in range(3):
                    opposite = lax.rem(pos[ORD[p][2]] + 2, 4)
                    arrived(half_chunk(p, rel, opposite, 0), g3_s.at[p, rel, 2], g3_r.at[p, rel, 2])
                    arrived(half_chunk(p, rel, opposite, 1), g3_s.at[p, rel, 3], g3_r.at[p, rel, 3])
            to_sibling(2)

        s = lax.div(i, 2)
        d = jnp.where(s == 0, 0, jnp.where(s == 1, 3, jnp.where(s == 2, 1, 2)))
        odd = lax.rem(i, 2)
        half = jnp.where(odd == 0, c, 1 - c)

        @pl.when(odd == 1)
        def _():
            for p in range(3):
                arrived(gh[p].at[(1 - c,) + slab(p, d)], d_s.at[p, d], d_r.at[p, d])

        for p in range(3):
            idx = slab(p, d)
            rows = gh[p][(half,) + idx].reshape(256, CW[p])
            k = pl.ds(pl.multiple_of(half * HALF + OFF[p], 128), CW[p])
            sums = jnp.dot(rows, wgu[k, :], preferred_element_type=F32)
            acc[idx] += sums.reshape(4, 4, 16, 2 * EH)

    for k, d in enumerate(STEPS):
        view = share.at[:, :, lax.rem(z + 4 - d, 4), c]
        arrived(view, sh_s.at[2, k], sh_r.at[2, k])
    view = share.at[:, :, :, c]
    send(view, view, pair_s.at[3], pair_r.at[3], sib)
    arrived(share.at[:, :, :, 1 - c], pair_s.at[3], pair_r.at[3])

    expert = lax.div(me, 2)
    wide_lanes = lax.broadcasted_iota(jnp.int32, (64, 128), 1)

    @pl.loop(0, 16)
    def _(i):
        ix, iy = lax.div(i, 4), lax.rem(i, 4)
        weight = jnp.sum(
            jnp.where(wide_lanes == expert, share[ix, iy].reshape(64, 128), 0.0), axis=-1, keepdims=True
        )
        both = acc[ix, iy].reshape(64, 2 * EH)
        gate, up = both[:, :EH], both[:, EH:]
        active = gate / (1.0 + jnp.exp(-gate)) * up * weight
        act[c, ix, iy] = active.astype(BF16).reshape(4, 16, EH)

        @pl.when(iy == 3)
        def _():
            view = act.at[c, ix]
            remote(view, view, act_s.at[ix], act_r.at[ix], sib).start()

    for ix in range(4):
        arrived(act.at[1 - c, ix], act_s.at[ix], act_r.at[ix])
    arrived(wd.at[1 - c], pair_s.at[1], pair_r.at[1])

    halves = (pl.ds(0, 2), pl.ds(2, 2))

    def slab_part(p, d, first=slice(None), second=slice(None)):
        order = ORD[p]
        idx = [None] * 3
        idx[order[0]], idx[order[1]] = first, second
        idx[order[2]] = lax.rem(pos[order[2]] + d, 4)
        return tuple(idx)

    def near(p, stage, d):
        return device(shift(pos, ORD[p][stage], d), c)

    @pl.loop(0, 4)
    def _(s):
        d = jnp.where(s == 0, 2, jnp.where(s == 1, 1, jnp.where(s == 2, 3, 0)))
        for p in range(3):
            idx = slab(p, d)
            cols = pl.ds(OFF[p], CW[p])
            sums = jnp.dot(act[(0,) + idx].reshape(256, EH), wd[0, :, cols], preferred_element_type=F32)
            sums = sums + jnp.dot(act[(1,) + idx].reshape(256, EH), wd[1, :, cols], preferred_element_type=F32)
            part[p][idx] = sums.astype(BF16).reshape(4, 4, 16, CW[p])

            @pl.when(s == 0)
            def _():
                for h in range(2):
                    remote(
                        part[p].at[slab_part(p, 2, halves[h])], ra[p].at[h],
                        q3_s.at[p, h], q3_r.at[p, h], near(p, 2, 1 if h == 0 else 3),
                    ).start()

            @pl.when(s == 1)
            def _():
                remote(
                    part[p].at[slab_part(p, 1, halves[1])], rx[p].at[0, 1],
                    q3_s.at[p, 2], q3_r.at[p, 2], near(p, 2, 1),
                ).start()

            @pl.when(s == 2)
            def _():
                remote(
                    part[p].at[slab_part(p, 3, halves[0])], rx[p].at[1, 0],
                    q3_s.at[p, 3], q3_r.at[p, 3], near(p, 2, 3),
                ).start()

    for p in range(3):
        arrived(ra[p].at[0], q3_s.at[p, 0], q3_r.at[p, 0])
        idx = slab_part(p, 1, halves[0])
        part[p][idx] = (part[p][idx].astype(F32) + ra[p][0].astype(F32)).astype(BF16)
        send(part[p].at[idx], rx[p].at[0, 0], q3_s.at[p, 4], q3_r.at[p, 4], near(p, 2, 1))
        arrived(ra[p].at[1], q3_s.at[p, 1], q3_r.at[p, 1])
        idx = slab_part(p, 3, halves[1])
        part[p][idx] = (part[p][idx].astype(F32) + ra[p][1].astype(F32)).astype(BF16)
        send(part[p].at[idx], rx[p].at[1, 1], q3_s.at[p, 5], q3_r.at[p, 5], near(p, 2, 3))
    for p in range(3):
        arrived(rx[p].at[0, 1], q3_s.at[p, 2], q3_r.at[p, 2])
        arrived(rx[p].at[1, 0], q3_s.at[p, 3], q3_r.at[p, 3])
        arrived(rx[p].at[0, 0], q3_s.at[p, 4], q3_r.at[p, 4])
        arrived(rx[p].at[1, 1], q3_s.at[p, 5], q3_r.at[p, 5])
        for h in range(2):
            idx = slab_part(p, 0, halves[h])
            part[p][idx] = (
                part[p][idx].astype(F32) + rx[p][0, h].astype(F32) + rx[p][1, h].astype(F32)
            ).astype(BF16)
        b = ORD[p][1]
        for k, d in enumerate(STEPS):
            line = slab_part(p, 0, slice(None), lax.rem(pos[b] + d, 4))
            send(part[p].at[line], ry[p].at[k], q1_s.at[p, 0, k], q1_r.at[p, 0, k], near(p, 1, d))
    for p in range(3):
        a, b = ORD[p][0], ORD[p][1]
        line = slab_part(p, 0, slice(None), pos[b])
        total = part[p][line].astype(F32)
        for k in range(3):
            arrived(ry[p].at[k], q1_s.at[p, 0, k], q1_r.at[p, 0, k])
            total = total + ry[p][k].astype(F32)
        part[p][line] = total.astype(BF16)
        for k, d in enumerate(STEPS):
            spot = slab_part(p, 0, lax.rem(pos[a] + d, 4), pos[b])
            send(part[p].at[spot], rz[p].at[k], q1_s.at[p, 1, k], q1_r.at[p, 1, k], near(p, 0, d))
    pieces = []
    for p in range(3):
        total = part[p][pos].astype(F32)
        for k in range(3):
            arrived(rz[p].at[k], q1_s.at[p, 1, k], q1_r.at[p, 1, k])
            total = total + rz[p][k].astype(F32)
        pieces.append(total)
    mixed = (kept[...] + jnp.concatenate(pieces, axis=1)).astype(BF16).astype(F32)
    fin_tx[...] = jnp.where(first, mixed[8:], mixed[:8])
    send(fin_tx, fin_rx, pair_s.at[4], pair_r.at[4], sib)
    out[:, own_cols] = jnp.where(first, mixed[:8], mixed[8:]).astype(BF16)
    arrived(fin_rx, pair_s.at[4], pair_r.at[4])
    out[:, other_cols] = fin_rx[...].astype(BF16)

    for copy in sends:
        copy.wait_send()

    def sent(view, ssem, rsem):
        remote(view, view, ssem, rsem, sib).wait_send()

    for p in range(3):
        for rel in range(4):
            for half in range(2):
                view = half_chunk(p, rel, pos[ORD[p][2]], half)
                sent(view, g3_s.at[p, rel, 2 + half], g3_r.at[p, rel, 2 + half])
        for d in range(4):
            sent(block(p, slab(p, 0)), d_s.at[p, d], d_r.at[p, d])
    for ix in range(4):
        sent(act.at[c, ix], act_s.at[ix], act_r.at[ix])
    for p in range(3):
        for k, d in enumerate((2, 2, 1, 3)):
            sent(part[p].at[slab_part(p, d, halves[0])], q3_s.at[p, k], q3_r.at[p, k])


def local(
    residual, queries, key_cache, value_cache, new_keys, new_values, lengths, out_weight, norm_gain,
    routes, gate_probs, w_gate, w_up, w_down,
):
    vm = pl.BlockSpec(memory_space=pltpu.VMEM)
    hbm = pl.BlockSpec(memory_space=pl.ANY)
    dma = pltpu.SemaphoreType.DMA

    def v(*shape, dtype=BF16):
        return pltpu.VMEM(shape, dtype)

    def slab_shape(p, first, second):
        spec = {ORD[p][0]: first, ORD[p][1]: second}
        return tuple(spec[axis] for axis in range(3) if axis != ORD[p][2])

    scratch = [
        v(ROWS, CACHE, KVH * HD), v(ROWS, CACHE, KVH * HD), v(1024, HALF), v(D, 2 * EH), v(2, EH, HALF),
        v(8, 64, HD), v(8, 2, 64, HD), v(128, 1024), v(8, 16, HALF), v(8, 16, HALF),
        v(8, HALF, dtype=F32), v(8, HALF, dtype=F32), v(16, 128, dtype=F32), v(16, 128, dtype=F32),
        v(4, 4, 4, 2, 8, 128, dtype=F32),
        *[v(2, 4, 4, 4, 16, w) for w in CW],
        v(4, 4, 4, 16, 2 * EH, dtype=F32), v(2, 4, 4, 4, 16, EH),
        *[v(4, 4, 4, 16, w) for w in CW],
        *[v(2, *slab_shape(p, 2, 4), 16, CW[p]) for p in range(3)],
        *[v(2, 2, *slab_shape(p, 2, 4), 16, CW[p]) for p in range(3)],
        *[v(3, 4, 16, w) for w in CW],
        *[v(3, 16, w) for w in CW],
        v(16, HALF, dtype=F32), v(8, HALF, dtype=F32), v(8, HALF, dtype=F32),
        dma((7,)), dma((5,)), dma((5,)), dma((8,)), dma((8,)), dma((8,)), dma((8,)), dma((4, 8)), dma((4, 8)),
        dma((3, 3)), dma((3, 3)),
        dma((3, 2, 3)), dma((3, 2, 3)), dma((3, 4, 4)), dma((3, 4, 4)), dma((3, 4)), dma((3, 4)),
        dma((4,)), dma((4,)), dma((3, 6)), dma((3, 6)), dma((3, 2, 3)), dma((3, 2, 3)),
    ]
    return pl.pallas_call(
        kernel,
        out_shape=jax.ShapeDtypeStruct((ROWS, D), BF16),
        in_specs=[vm, vm, hbm, hbm, vm, vm, pl.BlockSpec(memory_space=pltpu.SMEM), hbm, vm, vm, vm, hbm, hbm, hbm],
        out_specs=vm,
        scratch_shapes=scratch,
        compiler_params=pltpu.CompilerParams(
            collective_id=0, has_side_effects=True, vmem_limit_bytes=58 * 2**20
        ),
        cost_estimate=pl.CostEstimate(flops=12 * 10**9, bytes_accessed=24 * 2**20, transcendentals=10**6),
    )(
        residual, queries, key_cache, value_cache, new_keys, new_values, lengths, out_weight,
        norm_gain.reshape(1, D), routes, gate_probs, w_gate, w_up, w_down,
    )


def solution(mesh):
    both = ("wide", "narrow")
    rows, cubes = P(both, None), P(both, None, None)
    in_specs = (
        rows, rows, cubes, cubes, rows, rows, P(both), P("narrow", None), P(), rows, rows, cubes, cubes, cubes,
    )
    return jax.shard_map(local, mesh=mesh, in_specs=in_specs, out_specs=rows, check_vma=False)
```

time: 221 us -> 93.8 us (0.42)
  waiting for transfers between devices: 95.5 us -> 0 us
  Pallas kernels: 0 us -> 92.2 us
  blocking collectives: 51.9 us -> 0 us
  local copies, waits for them, and re-layouts: 23.6 us -> 1.47 us
  matrix products: 17 us -> 0 us
  between operations: 13.6 us -> 0.01 us
  other arithmetic: 12.1 us -> 0 us
  starting transfers between devices: 6.74 us -> 0 us
    pallas_call x0 -> x1, Pallas kernels: none -> 92.2 us  [local(): pl.pallas_call(kernel, out_shape=jax.ShapeDtypeStruct((ROWS, D), BF16), i...]
    reduce_scatter x1 -> x0, waiting for transfers between devices: 67.6 us -> none  [local(): lax.psum_scatter(jnp.dot(heads_local, out_weight, preferred_element_type=...]
    all_to_all x2 -> x0, blocking collectives: 51.9 us -> none  [the longest x1 37.6 us: local(): lax.all_to_all(packed, ('wide', 'narrow'), split_axis=0, concat_axis=0, t...]
    all_to_all x1 -> x0, waiting for transfers between devices: 27.9 us -> none  [local(): lax.all_to_all(part_sums.astype(jnp.bfloat16), ('wide', 'narrow'), split_...]
    dot_general x7 -> x0, matrix products: 17 us -> none  [the longest x1 5.78 us: local(): jnp.dot(heads_local, out_weight, preferred_element_type=jnp.float32)]
    reduce_sum x6 -> x0, other arithmetic: 9.32 us -> none  [the longest x1 6.26 us: local(): jnp.sum(returned.reshape(experts, 2, capacity, D), axis=1)]
    all_to_all x1 -> x0, starting transfers between devices: 6.74 us -> none  [local(): lax.all_to_all(part_sums.astype(jnp.bfloat16), ('wide', 'narrow'), split_...]
    broadcast_in_dim x2 -> x0, local copies, waits for them, and re-layouts: 6.25 us -> none  [local(): jnp.broadcast_to(packed.reshape(experts, 1, capacity, D), (experts, 2, ca...]
  transfers between devices with their start and end apart: 2 -> 0, of which waited for: 2 -> 0; matrix products, arithmetic and copies ran while one was open for 0% -> 0% of each run, Pallas kernels for 0% -> 0%
where the time goes in v1:
time: 93.8 us; the launch traced here: 93.7 us
  Pallas kernels  92.2 us (98%)
  local copies, waits for them, and re-layouts  1.47 us (2%)
    pallas_call x1, Pallas kernels, local(): pl.pallas_call(kernel, out_shape=jax.ShapeDtypeStruct((ROWS, D), BF16), i...  92.2 us

profile of v1, /device:TPU:1, one launch (start us, length us, event | category | flops | bytes accessed | tf_op | source)
XLA Modules:
  0.0 93.7 jit_solution(15325269339046750507)
XLA Ops:
  0.0 92.2 %shard_map.136 = bf16[8,4096]{1,0:T(8,128)(2,1)} custom-call(bf16[8,4096]{1,0:T(8,128)(2,1)} %residual.1, bf16[8,8192]{1,0:T(8,128)(2,1)} %queries.1, bf16[8,256,512]{2,1,0:T(8,128)(2,1)} %key_cache.1, bf16[8,256,512]{2,1,0:T(8,128)(2,1)} %value_cache.1, bf16[8,512]{1,0:T(8,128)(2,1)} %new_keys.1, bf16[8,512]{1,0:T(8,128)(2,1)} %new_values.1, s32[8]{0:T(128)} %lengths.1, ...), custom_call_target="tpu_custom_call" | custom-call | flops 12000000000 | bytes 25165824 | tf_op jit(solution)/shard_map/pallas_call | solution.py:525
  92.2 1.5 %copy.16 = bf16[8,4096]{1,0:T(8,128)(2,1)} copy(bf16[8,4096]{1,0:T(8,128)(2,1)} %shard_map.136) | data formatting | bytes 131072

commit v2 on v1

v2 whole, which is shorter than its diff:
```python
import functools

import jax
import jax.numpy as jnp
from jax import lax
from jax.experimental import pallas as pl
from jax.experimental.pallas import tpu as pltpu
from jax.sharding import PartitionSpec as P

MESH = pl.DeviceIdType.MESH
F32 = jnp.float32
BF16 = jnp.bfloat16

D = 4096
HALF = 2048
HQ = 64
KVH = 4
HD = 128
TOP = 8
CACHE = 256
ROWS = 8
EH = 384

CW = (640, 640, 768)
OFF = (0, 640, 1280)
ORD = ((0, 1, 2), (1, 2, 0), (2, 0, 1))
STEPS = (1, 3, 2)


def coords():
    w, n = lax.axis_index("wide"), lax.axis_index("narrow")
    c = lax.rem(w, 2)
    z = lax.rem(lax.div(w, 2), 4)
    x = lax.div(n, 4) * 2 + lax.div(w, 8)
    return (x, lax.rem(n, 4), z), c, w * 8 + n, n


def device(pos, c):
    x, y, z = pos
    return (lax.rem(x, 2) * 8 + z * 2 + c, lax.div(x, 2) * 4 + y)


def shift(pos, axis, d):
    moved = list(pos)
    moved[axis] = lax.rem(moved[axis] + d, 4)
    return tuple(moved)


def remote(src, dst, ssem, rsem, target):
    return pltpu.make_async_remote_copy(
        src_ref=src, dst_ref=dst, send_sem=ssem, recv_sem=rsem, device_id=target, device_id_type=MESH
    )


def slab_index(p, first=slice(None), second=slice(None)):
    order = ORD[p]
    spec = {order[0]: first, order[1]: second}
    return tuple(spec[axis] for axis in range(3) if axis != order[2])


def kernel(
    residual_in, queries_in, key_cache, value_cache, new_keys_in, new_values_in, lengths_in, out_weight, gain_in,
    routes_in, probs_in, w_gate, w_up, w_down,
    out,
    residual, queries, new_keys, new_values, lengths, norm_gain, routes, gate_probs,
    keys, values, wo, wgu, wd, att, att_rx, a_mat, y_tx, y_rx, res_tx, res_rx, sq_tx, sq_rx,
    table, plane0, plane1, plane2, sel, perm, unperm, weight, stx0, stx1, stx2, srx0, srx1, srx2, acc, act,
    utx0, utx1, utx2, urx0, urx1, urx2, ltx0, ltx1, ltx2, lrx0, lrx1, lrx2, line0, line1, line2,
    btx0, btx1, btx2, brx0, brx1, brx2, kept, fin_tx, fin_rx,
    lsem, small, pair_s, pair_r, a2a_s, a2a_r, af_s, af_r, y_s, y_r, sh_s, sh_r,
    g1_s, g1_r, g2_s, g2_r, g3_s, g3_r, q3_s, q3_r, q2_s, q2_r, q1_s, q1_r,
):
    pos, c, me, n_me = coords()
    x, y, z = pos
    sib = device(pos, 1 - c)
    plane = (plane0, plane1, plane2)
    stx, srx, utx, urx = (stx0, stx1, stx2), (srx0, srx1, srx2), (utx0, utx1, utx2), (urx0, urx1, urx2)
    ltx, lrx, line = (ltx0, ltx1, ltx2), (lrx0, lrx1, lrx2), (line0, line1, line2)
    btx, brx = (btx0, btx1, btx2), (brx0, brx1, brx2)
    own_cols = pl.ds(pl.multiple_of(c * HALF, HALF), HALF)
    other_cols = pl.ds(pl.multiple_of((1 - c) * HALF, HALF), HALF)
    sends = []

    def send(src, dst, ssem, rsem, target, keep=True):
        copy = remote(src, dst, ssem, rsem, target)
        copy.start()
        if keep:
            sends.append(copy)

    def arrived(dst, ssem, rsem):
        remote(dst, dst, ssem, rsem, sib).wait_recv()

    group = [(dx, dy) for dx in range(2) for dy in range(4)]

    def member(dx, dy):
        gx = x if dx == 0 else 3 - x
        gy = lax.rem(y + dy, 4)
        return (gx, gy, z), lax.div(gx, 2) * 4 + gy

    local = [
        pltpu.make_async_copy(key_cache, keys, lsem.at[0]),
        pltpu.make_async_copy(value_cache, values, lsem.at[1]),
        pltpu.make_async_copy(out_weight.at[:, own_cols], wo, lsem.at[2]),
        pltpu.make_async_copy(w_gate.at[0], wgu.at[:, pl.ds(0, EH)], lsem.at[3]),
        pltpu.make_async_copy(w_up.at[0], wgu.at[:, pl.ds(EH, EH)], lsem.at[4]),
        pltpu.make_async_copy(w_down.at[0], wd, lsem.at[5]),
    ]
    arguments = [
        pltpu.make_async_copy(src, dst, small.at[i])
        for i, (src, dst) in enumerate((
            (routes_in, routes), (probs_in, gate_probs), (residual_in, residual), (lengths_in, lengths),
            (queries_in, queries), (new_keys_in, new_keys), (new_values_in, new_values), (gain_in, norm_gain),
        ))
    ]
    for copy in arguments:
        copy.start()
    for copy in local[:3]:
        copy.start()

    barrier = pltpu.get_barrier_semaphore()
    partners = [sib] + [device(shift(pos, a, d), c) for a in range(3) for d in STEPS]
    partners += [device(shift(pos, a, d), 1 - c) for a in range(3) for d in STEPS]
    partners += [device(member(1, dy)[0], c) for dy in (1, 2, 3)]
    for partner in partners:
        pl.semaphore_signal(barrier, inc=1, device_id=partner, device_id_type=MESH)

    for copy in arguments[:3]:
        copy.wait()
    probs = gate_probs[...]
    shares = probs / jnp.sum(probs, axis=-1, keepdims=True)
    lanes = lax.broadcasted_iota(jnp.int32, (ROWS, 128), 1)
    dense = jnp.zeros((ROWS, 128), F32)
    named = jnp.zeros((ROWS, 128), F32)
    chosen = routes[...]
    for k in range(TOP):
        hit = chosen[:, k : k + 1] == lanes
        dense = dense + jnp.where(hit, shares[:, k : k + 1], 0.0)
        named = named + jnp.where(hit, 1.0, 0.0)
    earlier, running = [], jnp.zeros((1, 128), F32)
    for t in range(ROWS):
        earlier.append(running)
        running = running + named[t : t + 1]
    earlier = jnp.concatenate(earlier, axis=0)
    number = lax.broadcasted_iota(jnp.int32, (ROWS, 128), 0).astype(F32) + 1.0
    entries = []
    for value in (number, dense):
        for r in range(2):
            taken = jnp.where(earlier == float(r), named * value, 0.0)
            entries.append(jnp.sum(taken, axis=0, keepdims=True) - (1.0 if value is number else 0.0))
    table[x, y, z, c] = jnp.concatenate(entries + [jnp.zeros((4, 128), F32)], axis=0)
    res_tx[...] = residual[:, other_cols].astype(F32)


    local[0].wait()
    local[1].wait()
    for copy in local[3:]:
        copy.start()
    for copy in arguments[3:]:
        copy.wait()
    scaling = HD ** (-0.5)
    row_request = lax.rem(lax.broadcasted_iota(jnp.int32, (128, CACHE), 0), ROWS)
    limit = jnp.zeros((128, CACHE), jnp.int32)
    for r in range(ROWS):
        limit = jnp.where(row_request == r, lengths[r], limit)
    visible = lax.broadcasted_iota(jnp.int32, (128, CACHE), 1) < limit
    for g in range(KVH):
        cols = slice(g * HD, (g + 1) * HD)
        q = jnp.concatenate(
            [queries[:, (g * 16 + h) * HD : (g * 16 + h + 1) * HD].astype(F32) for h in range(16)], axis=0
        )
        scores = lax.dot_general(
            q.astype(BF16), keys[:, :, cols].reshape(ROWS * CACHE, HD), (((1,), (1,)), ((), ())),
            preferred_element_type=F32,
        )
        picked = scores[:, :CACHE]
        for r in range(1, ROWS):
            picked = jnp.where(row_request == r, scores[:, r * CACHE : (r + 1) * CACHE], picked)
        picked = jnp.where(visible, picked * scaling, -jnp.inf)
        fresh = jnp.concatenate([new_keys[:, cols].astype(F32)] * 16, axis=0)
        own = jnp.sum(q * fresh, axis=-1, keepdims=True) * scaling
        highest = jnp.maximum(jnp.max(picked, axis=-1, keepdims=True), own)
        weights = jnp.exp(picked - highest)
        own = jnp.exp(own - highest)
        norm = jnp.sum(weights, axis=-1, keepdims=True) + own
        weights = weights / norm
        own = (own / norm).astype(BF16).astype(F32)
        spread = jnp.concatenate(
            [jnp.where(row_request == r, weights, 0.0).astype(BF16) for r in range(ROWS)], axis=1
        )
        got = jnp.dot(spread, values[:, :, cols].reshape(ROWS * CACHE, HD), preferred_element_type=F32)
        got = got + own * jnp.concatenate([new_values[:, cols].astype(F32)] * 16, axis=0)
        att[2 * g : 2 * g + 2] = got.astype(BF16).reshape(2, 64, HD)

    pl.semaphore_wait(barrier, len(partners))
    mine = pltpu.make_async_copy(att.at[n_me], att_rx.at[n_me, c], lsem.at[6])
    mine.start()
    for i, (dx, dy) in enumerate(group):
        if i:
            target, n = member(dx, dy)
            send(att.at[n], att_rx.at[n_me, c], a2a_s.at[i], a2a_r.at[i], device(target, c))
    send(res_tx, res_rx, pair_s.at[0], pair_r.at[0], sib)
    for k, d in enumerate(STEPS):
        view = table.at[x, y, z, c]
        send(view, view, sh_s.at[0, k], sh_r.at[0, k], device(shift(pos, 0, d), c))
    mine.wait()
    for i, (dx, dy) in enumerate(group):
        _, n = member(dx, (4 - dy) % 4)
        view = att_rx.at[n, c]
        if i:
            arrived(view, a2a_s.at[i], a2a_r.at[i])
        send(view, view, af_s.at[i], af_r.at[i], sib)
    for i, (dx, dy) in enumerate(group):
        _, n = member(dx, (4 - dy) % 4)
        arrived(att_rx.at[n, 1 - c], af_s.at[i], af_r.at[i])

    for k, d in enumerate(STEPS):
        view = table.at[lax.rem(x + 4 - d, 4), y, z, c]
        arrived(view, sh_s.at[0, k], sh_r.at[0, k])
    for k, d in enumerate(STEPS):
        view = table.at[:, y, z, c]
        send(view, view, sh_s.at[1, k], sh_r.at[1, k], device(shift(pos, 1, d), c))
    heads = att_rx[...].astype(F32).reshape(16, 64, HD)
    for h in range(8):
        a_mat[:, h * HD : (h + 1) * HD] = heads[:, h * 8 : (h + 1) * 8].reshape(128, HD).astype(BF16)

    local[2].wait()
    for j in range(4):
        cols = pl.ds(j * 512, 512)
        sums = jnp.dot(a_mat[...], wo[:, cols], preferred_element_type=F32)
        y_tx[:, :, cols] = sums.astype(BF16).reshape(8, 16, 512)
        for i, (dx, dy) in enumerate(group):
            if i:
                target, n = member(dx, dy)
                send(y_tx.at[n, :, cols], y_rx.at[i, :, cols], y_s.at[j, i], y_r.at[j, i], device(target, c))
    for k, d in enumerate(STEPS):
        view = table.at[:, lax.rem(y + 4 - d, 4), z, c]
        arrived(view, sh_s.at[1, k], sh_r.at[1, k])
    for k, d in enumerate(STEPS):
        view = table.at[:, :, z, c]
        send(view, view, sh_s.at[2, k], sh_r.at[2, k], device(shift(pos, 2, d), c))

    big_r = lax.broadcasted_iota(jnp.int32, (256, 256), 0)
    big_c = lax.broadcasted_iota(jnp.int32, (256, 256), 1)

    def common(i, p):
        digits = {ORD[p][2]: lax.div(i, 64), ORD[p][1]: lax.rem(lax.div(i, 16), 4), ORD[p][0]: lax.rem(lax.div(i, 4), 4)}
        return digits[2] * 64 + digits[1] * 16 + digits[0] * 4 + lax.rem(i, 4)

    for p in (1, 2):
        perm[p - 1] = jnp.where(big_r == common(big_c, p), 1.0, 0.0).astype(BF16)
        unperm[p - 1] = jnp.where(common(big_r, p) == big_c, 1.0, 0.0).astype(BF16)
    arrived(res_rx, pair_s.at[0], pair_r.at[0])
    own_res, other_res = residual[:, own_cols].astype(F32), res_rx[...]
    first = c == 0
    total = jnp.concatenate(
        [jnp.where(first, own_res, other_res), jnp.where(first, other_res, own_res)], axis=0
    )
    attention = y_tx[n_me].astype(F32)
    for i in range(1, 8):
        for j in range(4):
            arrived(y_rx.at[i, :, pl.ds(j * 512, 512)], y_s.at[j, i], y_r.at[j, i])
        attention = attention + y_rx[i].astype(F32)
    for k, d in enumerate(STEPS):
        view = table.at[:, :, lax.rem(z + 4 - d, 4), c]
        arrived(view, sh_s.at[2, k], sh_r.at[2, k])
    view = table.at[:, :, :, c]
    send(view, view, pair_s.at[3], pair_r.at[3], sib)
    stream = (total + attention).astype(BF16).astype(F32)
    squares = jnp.sum(stream * stream, axis=-1, keepdims=True)
    sq_tx[...] = jnp.broadcast_to(squares, (16, 128))
    send(sq_tx, sq_rx, pair_s.at[2], pair_r.at[2], sib)
    kept[...] = stream
    arrived(sq_rx, pair_s.at[2], pair_r.at[2])
    mean = (squares + sq_rx[:, 0:1]) * (1.0 / D)
    normed = (stream * lax.rsqrt(mean + 1e-06) * norm_gain[:, own_cols]).astype(BF16)
    for p in range(3):
        plane[p][slab_index(p, pos[ORD[p][0]], pos[ORD[p][1]])] = normed[:, OFF[p] : OFF[p] + CW[p]]

    def at(p, first, second):
        return plane[p].at[slab_index(p, first, second)]

    def near(p, stage, d, core=c):
        return device(shift(pos, ORD[p][stage], d), core)

    def coordinate(p, stage, d):
        return lax.rem(pos[ORD[p][stage]] + d, 4)

    def along(p, i, d):
        return coordinate(p, 0, 0 if i == 0 else 4 - STEPS[i - 1]), coordinate(p, 1, d)

    def spread_block(p, i):
        view = at(p, *along(p, i, 0))
        for k, d in enumerate(STEPS):
            send(view, view, g2_s.at[p, i, k], g2_r.at[p, i, k], near(p, 1, d))

    for p in range(3):
        view = at(p, *along(p, 0, 0))
        for k, d in enumerate(STEPS):
            send(view, view, g1_s.at[p, k], g1_r.at[p, k], near(p, 0, d))
    for p in range(3):
        spread_block(p, 0)

    arrived(table.at[:, :, :, 1 - c], pair_s.at[3], pair_r.at[3])
    slot = lax.broadcasted_iota(jnp.int32, (16, 64), 0)
    token = lax.broadcasted_iota(jnp.int32, (16, 64), 1)
    same = lax.div(slot, 2) == lax.div(token, 8)
    place = lax.rem(token, 8)
    take_token = jnp.where(same & (place == lax.rem(slot, 2)), 1.0, 0.0).astype(BF16)
    take_share = jnp.where(same & (place == lax.rem(slot, 2) + 2), 1.0, 0.0).astype(BF16)
    place = place.astype(F32)
    lane16 = lax.broadcasted_iota(jnp.int32, (16, 128), 1)

    def expert_of(where, core):
        ex, ey, ez = where
        return lax.div(((lax.rem(ex, 2) * 8 + ez * 2 + core) * 8) + lax.div(ex, 2) * 4 + ey, 2)

    for p in range(3):
        for rel in range(4):
            idx = list(pos)
            idx[ORD[p][0]], idx[ORD[p][1]] = slice(None), coordinate(p, 1, rel)
            entries = table[tuple(idx)].reshape(64, 128).astype(BF16)
            numbers = jnp.dot(take_token, entries, preferred_element_type=F32)
            for q in range(4):
                chip = list(pos)
                chip[ORD[p][2]] = q
                for core in range(2):
                    wanted = jnp.sum(
                        jnp.where(lane16 == expert_of(chip, core), numbers, 0.0), axis=-1, keepdims=True
                    )
                    hits = jnp.where(same & (wanted == place), 1.0, 0.0)
                    sel[p, rel, (q * 2 + core) * 16 : (q * 2 + core + 1) * 16] = hits.astype(BF16)

    def dispatch(p, rel):
        rows = plane[p][slab_index(p, slice(None), coordinate(p, 1, rel))].reshape(64, CW[p])
        picked = jnp.dot(sel[p, rel], rows, preferred_element_type=F32).astype(BF16)
        stx[p][rel] = picked.reshape(4, 2, 16, CW[p])
        a3, a2 = coordinate(p, 2, 0), coordinate(p, 1, rel)
        spot = srx[p].at[c, a3, a2]
        for dq in STEPS:
            for core in range(2):
                send(
                    stx[p].at[rel, coordinate(p, 2, dq), core], spot,
                    g3_s.at[p, rel, dq, core], g3_r.at[p, rel, dq, c], near(p, 2, dq, core),
                )
        send(stx[p].at[rel, a3, 1 - c], spot, g3_s.at[p, rel, 0, 0], g3_r.at[p, rel, 0, 0], sib)
        srx[p][c, a3, a2] = stx[p][rel, a3, c]

    for k, d in enumerate(STEPS):
        for p in range(3):
            arrived(at(p, *along(p, k + 1, 0)), g1_s.at[p, k], g1_r.at[p, k])
            spread_block(p, k + 1)
    for p in range(3):
        dispatch(p, 0)
    for k, d in enumerate(STEPS):
        for p in range(3):
            for i in range(4):
                arrived(at(p, *along(p, i, 4 - d)), g2_s.at[p, i, k], g2_r.at[p, i, k])
            dispatch(p, 4 - d)

    mine_expert = lax.div(me, 2)

    @pl.loop(0, 16)
    def _(i):
        entries = table[:, lax.rem(i, 4), lax.div(i, 4)].reshape(64, 128)
        high = entries.astype(BF16)
        low = (entries - high.astype(F32)).astype(BF16)
        values = jnp.dot(take_share, high, preferred_element_type=F32)
        values = values + jnp.dot(take_share, low, preferred_element_type=F32)
        found = jnp.sum(jnp.where(lane16 == mine_expert, values, 0.0), axis=-1, keepdims=True)
        weight[i] = jnp.broadcast_to(found, (16, 128))

    for copy in local[3:]:
        copy.wait()

    for p in range(3):
        for rel in (0, 3, 1, 2):
            a2 = coordinate(p, 1, rel)
            for dq in STEPS:
                for core in range(2):
                    arrived(
                        srx[p].at[core, coordinate(p, 2, 4 - dq), a2],
                        g3_s.at[p, rel, dq, core], g3_r.at[p, rel, dq, core],
                    )
            arrived(srx[p].at[1 - c, coordinate(p, 2, 0), a2], g3_s.at[p, rel, 0, 0], g3_r.at[p, rel, 0, 0])
        for half in range(2):
            rows = srx[p][half].reshape(256, CW[p])
            if p:
                rows = jnp.dot(perm[p - 1], rows, preferred_element_type=F32).astype(BF16)
            k = slice(half * HALF + OFF[p], half * HALF + OFF[p] + CW[p])
            sums = jnp.dot(rows, wgu[k, :], preferred_element_type=F32)
            acc[...] = sums if p == 0 and half == 0 else acc[...] + sums
    gate, up = acc[:, :EH], acc[:, EH:]
    shares = weight[...].reshape(256, 128)[:, 0:1]
    active = (gate / (1.0 + jnp.exp(-gate)) * up * shares).astype(BF16)
    act[0] = active
    for p in (1, 2):
        act[p] = jnp.dot(unperm[p - 1], active, preferred_element_type=F32).astype(BF16)

    def give_back(p, half, rel):
        a3, a2 = coordinate(p, 2, 0), coordinate(p, 1, rel)
        spot = urx[p].at[a2, a3, c]
        for dq in STEPS:
            send(
                utx[p].at[half, coordinate(p, 2, dq), a2], spot,
                q3_s.at[p, rel, dq, half], q3_r.at[p, rel, dq, c], near(p, 2, dq, half),
            )

    for half in range(2):
        for p in range(3):
            cols = slice(half * HALF + OFF[p], half * HALF + OFF[p] + CW[p])
            sums = jnp.dot(act[p], wd[:, cols], preferred_element_type=F32)
            utx[p][half] = sums.astype(BF16).reshape(4, 4, 16, CW[p])
            give_back(p, half, 2)
    for rel in (2, 1, 3, 0):
        for p in range(3):
            a3, a2 = coordinate(p, 2, 0), coordinate(p, 1, rel)
            if rel != 2:
                for half in range(2):
                    give_back(p, half, rel)
            send(utx[p].at[1 - c, a3, a2], urx[p].at[a2, a3, c], q3_s.at[p, rel, 0, 0], q3_r.at[p, rel, 0, 0], sib)
            urx[p][a2, a3, c] = utx[p][c, a3, a2]

    for rel in (2, 1, 3, 0):
        for p in range(3):
            a2 = coordinate(p, 1, rel)
            for dq in STEPS:
                for core in range(2):
                    arrived(
                        urx[p].at[a2, coordinate(p, 2, 4 - dq), core],
                        q3_s.at[p, rel, dq, core], q3_r.at[p, rel, dq, core],
                    )
            arrived(urx[p].at[a2, coordinate(p, 2, 0), 1 - c], q3_s.at[p, rel, 0, 0], q3_r.at[p, rel, 0, 0])
            sums = lax.dot_general(
                sel[p, rel], urx[p][a2].reshape(128, CW[p]), (((0,), (0,)), ((), ())), preferred_element_type=F32
            )
            if rel:
                ltx[p][rel - 1] = sums.astype(BF16).reshape(4, 16, CW[p])
                send(ltx[p].at[rel - 1], lrx[p].at[rel - 1], q2_s.at[p, rel - 1], q2_r.at[p, rel - 1], near(p, 1, rel))
            else:
                line[p][...] = sums.reshape(4, 16, CW[p])
    for p in range(3):
        total = line[p][...]
        for k in (1, 0, 2):
            arrived(lrx[p].at[k], q2_s.at[p, k], q2_r.at[p, k])
            total = total + lrx[p][k].astype(F32)
        line[p][...] = total
        btx[p][...] = total.astype(BF16)
        for k, d in enumerate(STEPS):
            send(btx[p].at[coordinate(p, 0, d)], brx[p].at[k], q1_s.at[p, k], q1_r.at[p, k], near(p, 0, d))
    pieces = []
    for p in range(3):
        total = line[p][coordinate(p, 0, 0)]
        for k in range(3):
            arrived(brx[p].at[k], q1_s.at[p, k], q1_r.at[p, k])
            total = total + brx[p][k].astype(F32)
        pieces.append(total)
    mixed = (kept[...] + jnp.concatenate(pieces, axis=1)).astype(BF16).astype(F32)
    fin_tx[...] = jnp.where(first, mixed[8:], mixed[:8])
    send(fin_tx, fin_rx, pair_s.at[4], pair_r.at[4], sib)
    out[:, own_cols] = jnp.where(first, mixed[:8], mixed[8:]).astype(BF16)
    arrived(fin_rx, pair_s.at[4], pair_r.at[4])
    out[:, other_cols] = fin_rx[...].astype(BF16)

    for copy in sends:
        copy.wait_send()


def local(
    residual, queries, key_cache, value_cache, new_keys, new_values, lengths, out_weight, norm_gain,
    routes, gate_probs, w_gate, w_up, w_down,
):
    vm = pl.BlockSpec(memory_space=pltpu.VMEM)
    hbm = pl.BlockSpec(memory_space=pl.ANY)
    dma = pltpu.SemaphoreType.DMA

    def v(*shape, dtype=BF16):
        return pltpu.VMEM(shape, dtype)

    scratch = [
        v(ROWS, D), v(ROWS, HQ * HD), v(ROWS, KVH * HD), v(ROWS, KVH * HD), pltpu.SMEM((ROWS,), jnp.int32),
        v(1, D, dtype=F32), v(ROWS, TOP, dtype=jnp.int32), v(ROWS, TOP, dtype=F32),
        v(ROWS, CACHE, KVH * HD), v(ROWS, CACHE, KVH * HD), v(1024, HALF), v(D, 2 * EH), v(EH, D),
        v(8, 64, HD), v(8, 2, 64, HD), v(128, 1024), v(8, 16, HALF), v(8, 16, HALF),
        v(8, HALF, dtype=F32), v(8, HALF, dtype=F32), v(16, 128, dtype=F32), v(16, 128, dtype=F32),
        v(4, 4, 4, 2, 8, 128, dtype=F32),
        *[v(4, 4, 16, w) for w in CW],
        v(3, 4, 128, 64), v(2, 256, 256), v(2, 256, 256), v(16, 16, 128, dtype=F32),
        *[v(4, 4, 2, 16, w) for w in CW],
        *[v(2, 4, 4, 16, w) for w in CW],
        v(256, 2 * EH, dtype=F32), v(3, 256, EH),
        *[v(2, 4, 4, 16, w) for w in CW],
        *[v(4, 4, 2, 16, w) for w in CW],
        *[v(3, 4, 16, w) for w in CW],
        *[v(3, 4, 16, w) for w in CW],
        *[v(4, 16, w, dtype=F32) for w in CW],
        *[v(4, 16, w) for w in CW],
        *[v(3, 16, w) for w in CW],
        v(16, HALF, dtype=F32), v(8, HALF, dtype=F32), v(8, HALF, dtype=F32),
        dma((7,)), dma((8,)), dma((5,)), dma((5,)), dma((8,)), dma((8,)), dma((8,)), dma((8,)), dma((4, 8)), dma((4, 8)),
        dma((3, 3)), dma((3, 3)), dma((3, 3)), dma((3, 3)), dma((3, 4, 3)), dma((3, 4, 3)),
        dma((3, 4, 4, 2)), dma((3, 4, 4, 2)), dma((3, 4, 4, 2)), dma((3, 4, 4, 2)),
        dma((3, 3)), dma((3, 3)), dma((3, 3)), dma((3, 3)),
    ]
    return pl.pallas_call(
        kernel,
        out_shape=jax.ShapeDtypeStruct((ROWS, D), BF16),
        in_specs=[hbm] * 14,
        out_specs=vm,
        scratch_shapes=scratch,
        compiler_params=pltpu.CompilerParams(
            collective_id=0, has_side_effects=True, vmem_limit_bytes=58 * 2**20
        ),
        cost_estimate=pl.CostEstimate(flops=12 * 10**9, bytes_accessed=24 * 2**20, transcendentals=10**6),
    )(
        residual, queries, key_cache, value_cache, new_keys, new_values, lengths, out_weight,
        norm_gain.reshape(1, D), routes, gate_probs, w_gate, w_up, w_down,
    )


def solution(mesh):
    both = ("wide", "narrow")
    rows, cubes = P(both, None), P(both, None, None)
    in_specs = (
        rows, rows, cubes, cubes, rows, rows, P(both), P("narrow", None), P(), rows, rows, cubes, cubes, cubes,
    )
    return jax.shard_map(local, mesh=mesh, in_specs=in_specs, out_specs=rows, check_vma=False)
```

time: 93.8 us -> 75.4 us (0.80)
  Pallas kernels: 92.2 us -> 73.7 us
    pallas_call x1, Pallas kernels: 92.2 us -> 73.7 us  [local(): pl.pallas_call(kernel, out_shape=jax.ShapeDtypeStruct((ROWS, D), BF16), i...]
where the time goes in v2:
time: 75.4 us; the launch traced here: 75.2 us
  Pallas kernels  73.7 us (98%)
  local copies, waits for them, and re-layouts  1.47 us (2%)
    pallas_call x1, Pallas kernels, local(): pl.pallas_call(kernel, out_shape=jax.ShapeDtypeStruct((ROWS, D), BF16), i...  73.7 us

profile of v2, /device:TPU:1, one launch (start us, length us, event | category | flops | bytes accessed | tf_op | source)
XLA Modules:
  0.0 75.2 jit_solution(2184084597810989490)
XLA Ops:
  0.0 73.7 %shard_map.136 = bf16[8,4096]{1,0:T(8,128)(2,1)} custom-call(bf16[8,4096]{1,0:T(8,128)(2,1)} %residual_in.1, bf16[8,8192]{1,0:T(8,128)(2,1)} %queries_in.1, bf16[8,256,512]{2,1,0:T(8,128)(2,1)} %key_cache.1, bf16[8,256,512]{2,1,0:T(8,128)(2,1)} %value_cache.1, bf16[8,512]{1,0:T(8,128)(2,1)} %new_keys_in.1, bf16[8,512]{1,0:T(8,128)(2,1)} %new_values_in.1, ...), custom_call_target="tpu_custom_call" | custom-call | flops 12000000000 | bytes 25165824 | tf_op jit(solution)/shard_map/pallas_call | solution.py:504
  73.8 1.5 %copy.16 = bf16[8,4096]{1,0:T(8,128)(2,1)} copy(bf16[8,4096]{1,0:T(8,128)(2,1)} %shard_map.136) | data formatting | bytes 131072

commit v3 on v2

--- a/solution.py
+++ b/solution.py
@@ -79,13 +79,13 @@
     btx, brx = (btx0, btx1, btx2), (brx0, brx1, brx2)
     own_cols = pl.ds(pl.multiple_of(c * HALF, HALF), HALF)
     other_cols = pl.ds(pl.multiple_of((1 - c) * HALF, HALF), HALF)
-    sends = []
-
-    def send(src, dst, ssem, rsem, target, keep=True):
-        copy = remote(src, dst, ssem, rsem, target)
-        copy.start()
-        if keep:
-            sends.append(copy)
+    few = pl.ds(0, 3)
+
+    def send(src, dst, ssem, rsem, target):
+        remote(src, dst, ssem, rsem, target).start()
+
+    def sent(src, ssem):
+        remote(src, src, ssem, ssem, sib).wait_send()
 
     def arrived(dst, ssem, rsem):
         remote(dst, dst, ssem, rsem, sib).wait_recv()
@@ -108,8 +108,8 @@
     arguments = [
         pltpu.make_async_copy(src, dst, small.at[i])
         for i, (src, dst) in enumerate((
-            (routes_in, routes), (probs_in, gate_probs), (residual_in, residual), (lengths_in, lengths),
-            (queries_in, queries), (new_keys_in, new_keys), (new_values_in, new_values), (gain_in, norm_gain),
+            (lengths_in, lengths), (queries_in, queries), (new_keys_in, new_keys), (new_values_in, new_values),
+            (routes_in, routes), (probs_in, gate_probs), (residual_in, residual), (gain_in, norm_gain),
         ))
     ]
     for copy in arguments:
@@ -124,38 +124,12 @@
     for partner in partners:
         pl.semaphore_signal(barrier, inc=1, device_id=partner, device_id_type=MESH)
 
-    for copy in arguments[:3]:
-        copy.wait()
-    probs = gate_probs[...]
-    shares = probs / jnp.sum(probs, axis=-1, keepdims=True)
-    lanes = lax.broadcasted_iota(jnp.int32, (ROWS, 128), 1)
-    dense = jnp.zeros((ROWS, 128), F32)
-    named = jnp.zeros((ROWS, 128), F32)
-    chosen = routes[...]
-    for k in range(TOP):
-        hit = chosen[:, k : k + 1] == lanes
-        dense = dense + jnp.where(hit, shares[:, k : k + 1], 0.0)
-        named = named + jnp.where(hit, 1.0, 0.0)
-    earlier, running = [], jnp.zeros((1, 128), F32)
-    for t in range(ROWS):
-        earlier.append(running)
-        running = running + named[t : t + 1]
-    earlier = jnp.concatenate(earlier, axis=0)
-    number = lax.broadcasted_iota(jnp.int32, (ROWS, 128), 0).astype(F32) + 1.0
-    entries = []
-    for value in (number, dense):
-        for r in range(2):
-            taken = jnp.where(earlier == float(r), named * value, 0.0)
-            entries.append(jnp.sum(taken, axis=0, keepdims=True) - (1.0 if value is number else 0.0))
-    table[x, y, z, c] = jnp.concatenate(entries + [jnp.zeros((4, 128), F32)], axis=0)
-    res_tx[...] = residual[:, other_cols].astype(F32)
-
 
     local[0].wait()
     local[1].wait()
     for copy in local[3:]:
         copy.start()
-    for copy in arguments[3:]:
+    for copy in arguments[:4]:
         copy.wait()
     scaling = HD ** (-0.5)
     row_request = lax.rem(lax.broadcasted_iota(jnp.int32, (128, CACHE), 0), ROWS)
@@ -197,28 +171,49 @@
     for i, (dx, dy) in enumerate(group):
         if i:
             target, n = member(dx, dy)
-            send(att.at[n], att_rx.at[n_me, c], a2a_s.at[i], a2a_r.at[i], device(target, c))
+            send(att.at[n], att_rx.at[n_me, c], a2a_s.at[0], a2a_r.at[i], device(target, c))
+    for copy in arguments[4:]:
+        copy.wait()
+    probs = gate_probs[...]
+    shares = probs / jnp.sum(probs, axis=-1, keepdims=True)
+    lanes = lax.broadcasted_iota(jnp.int32, (ROWS, 128), 1)
+    dense = jnp.zeros((ROWS, 128), F32)
+    named = jnp.zeros((ROWS, 128), F32)
+    chosen = routes[...]
+    for k in range(TOP):
+        hit = chosen[:, k : k + 1] == lanes
+        dense = dense + jnp.where(hit, shares[:, k : k + 1], 0.0)
+        named = named + jnp.where(hit, 1.0, 0.0)
+    earlier, running = [], jnp.zeros((1, 128), F32)
+    for t in range(ROWS):
+        earlier.append(running)
+        running = running + named[t : t + 1]
+    earlier = jnp.concatenate(earlier, axis=0)
+    number = lax.broadcasted_iota(jnp.int32, (ROWS, 128), 0).astype(F32) + 1.0
+    entries = []
+    for value in (number, dense):
+        for r in range(2):
+            taken = jnp.where(earlier == float(r), named * value, 0.0)
+            entries.append(jnp.sum(taken, axis=0, keepdims=True) - (1.0 if value is number else 0.0))
+    table[x, y, z, c] = jnp.concatenate(entries + [jnp.zeros((4, 128), F32)], axis=0)
+    res_tx[...] = residual[:, other_cols].astype(F32)
     send(res_tx, res_rx, pair_s.at[0], pair_r.at[0], sib)
-    for k, d in enumerate(STEPS):
+    for d in STEPS:
         view = table.at[x, y, z, c]
-        send(view, view, sh_s.at[0, k], sh_r.at[0, k], device(shift(pos, 0, d), c))
+        send(view, view, sh_s.at[0], sh_r.at[0], device(shift(pos, 0, d), c))
     mine.wait()
     for i, (dx, dy) in enumerate(group):
         _, n = member(dx, (4 - dy) % 4)
         view = att_rx.at[n, c]
         if i:
-            arrived(view, a2a_s.at[i], a2a_r.at[i])
-        send(view, view, af_s.at[i], af_r.at[i], sib)
-    for i, (dx, dy) in enumerate(group):
-        _, n = member(dx, (4 - dy) % 4)
-        arrived(att_rx.at[n, 1 - c], af_s.at[i], af_r.at[i])
-
-    for k, d in enumerate(STEPS):
-        view = table.at[lax.rem(x + 4 - d, 4), y, z, c]
-        arrived(view, sh_s.at[0, k], sh_r.at[0, k])
-    for k, d in enumerate(STEPS):
+            arrived(view, a2a_s.at[0], a2a_r.at[i])
+        send(view, view, af_s.at[0], af_r.at[0], sib)
+    arrived(att_rx.at[:, 1 - c], af_s.at[0], af_r.at[0])
+
+    arrived(table.at[few, y, z, c], sh_s.at[0], sh_r.at[0])
+    for d in STEPS:
         view = table.at[:, y, z, c]
-        send(view, view, sh_s.at[1, k], sh_r.at[1, k], device(shift(pos, 1, d), c))
+        send(view, view, sh_s.at[1], sh_r.at[1], device(shift(pos, 1, d), c))
     heads = att_rx[...].astype(F32).reshape(16, 64, HD)
     for h in range(8):
         a_mat[:, h * HD : (h + 1) * HD] = heads[:, h * 8 : (h + 1) * 8].reshape(128, HD).astype(BF16)
@@ -231,13 +226,11 @@
         for i, (dx, dy) in enumerate(group):
             if i:
                 target, n = member(dx, dy)
-                send(y_tx.at[n, :, cols], y_rx.at[i, :, cols], y_s.at[j, i], y_r.at[j, i], device(target, c))
-    for k, d in enumerate(STEPS):
-        view = table.at[:, lax.rem(y + 4 - d, 4), z, c]
-        arrived(view, sh_s.at[1, k], sh_r.at[1, k])
-    for k, d in enumerate(STEPS):
+                send(y_tx.at[n, :, cols], y_rx.at[i, :, cols], y_s.at[0], y_r.at[0], device(target, c))
+    arrived(table.at[:, few, z, c], sh_s.at[1], sh_r.at[1])
+    for d in STEPS:
         view = table.at[:, :, z, c]
-        send(view, view, sh_s.at[2, k], sh_r.at[2, k], device(shift(pos, 2, d), c))
+        send(view, view, sh_s.at[2], sh_r.at[2], device(shift(pos, 2, d), c))
 
     big_r = lax.broadcasted_iota(jnp.int32, (256, 256), 0)
     big_c = lax.broadcasted_iota(jnp.int32, (256, 256), 1)
@@ -256,13 +249,10 @@
         [jnp.where(first, own_res, other_res), jnp.where(first, other_res, own_res)], axis=0
     )
     attention = y_tx[n_me].astype(F32)
+    arrived(y_rx.at[pl.ds(1, 7)], y_s.at[0], y_r.at[0])
     for i in range(1, 8):
-        for j in range(4):
-            arrived(y_rx.at[i, :, pl.ds(j * 512, 512)], y_s.at[j, i], y_r.at[j, i])
         attention = attention + y_rx[i].astype(F32)
-    for k, d in enumerate(STEPS):
-        view = table.at[:, :, lax.rem(z + 4 - d, 4), c]
-        arrived(view, sh_s.at[2, k], sh_r.at[2, k])
+    arrived(table.at[:, :, few, c], sh_s.at[2], sh_r.at[2])
     view = table.at[:, :, :, c]
     send(view, view, pair_s.at[3], pair_r.at[3], sib)
     stream = (total + attention).astype(BF16).astype(F32)
@@ -291,12 +281,12 @@
     def spread_block(p, i):
         view = at(p, *along(p, i, 0))
         for k, d in enumerate(STEPS):
-            send(view, view, g2_s.at[p, i, k], g2_r.at[p, i, k], near(p, 1, d))
+            send(view, view, g2_s.at[p], g2_r.at[p, k], near(p, 1, d))
 
     for p in range(3):
         view = at(p, *along(p, 0, 0))
         for k, d in enumerate(STEPS):
-            send(view, view, g1_s.at[p, k], g1_r.at[p, k], near(p, 0, d))
+            send(view, view, g1_s.at[p], g1_r.at[p, k], near(p, 0, d))
     for p in range(3):
         spread_block(p, 0)
 
@@ -340,21 +330,20 @@
             for core in range(2):
                 send(
                     stx[p].at[rel, coordinate(p, 2, dq), core], spot,
-                    g3_s.at[p, rel, dq, core], g3_r.at[p, rel, dq, c], near(p, 2, dq, core),
+                    g3_s.at[p, 0], g3_r.at[p, 0], near(p, 2, dq, core),
                 )
-        send(stx[p].at[rel, a3, 1 - c], spot, g3_s.at[p, rel, 0, 0], g3_r.at[p, rel, 0, 0], sib)
+        send(stx[p].at[rel, a3, 1 - c], spot, g3_s.at[p, 1], g3_r.at[p, 1], sib)
         srx[p][c, a3, a2] = stx[p][rel, a3, c]
 
     for k, d in enumerate(STEPS):
         for p in range(3):
-            arrived(at(p, *along(p, k + 1, 0)), g1_s.at[p, k], g1_r.at[p, k])
+            arrived(at(p, *along(p, k + 1, 0)), g1_s.at[p], g1_r.at[p, k])
             spread_block(p, k + 1)
     for p in range(3):
         dispatch(p, 0)
     for k, d in enumerate(STEPS):
         for p in range(3):
-            for i in range(4):
-                arrived(at(p, *along(p, i, 4 - d)), g2_s.at[p, i, k], g2_r.at[p, i, k])
+            arrived(at(p, slice(None), coordinate(p, 1, 4 - d)), g2_s.at[p], g2_r.at[p, k])
             dispatch(p, 4 - d)
 
     mine_expert = lax.div(me, 2)
@@ -373,15 +362,8 @@
         copy.wait()
 
     for p in range(3):
-        for rel in (0, 3, 1, 2):
-            a2 = coordinate(p, 1, rel)
-            for dq in STEPS:
-                for core in range(2):
-                    arrived(
-                        srx[p].at[core, coordinate(p, 2, 4 - dq), a2],
-                        g3_s.at[p, rel, dq, core], g3_r.at[p, rel, dq, core],
-                    )
-            arrived(srx[p].at[1 - c, coordinate(p, 2, 0), a2], g3_s.at[p, rel, 0, 0], g3_r.at[p, rel, 0, 0])
+        arrived(srx[p].at[:, few], g3_s.at[p, 0], g3_r.at[p, 0])
+        arrived(srx[p].at[0, 0], g3_s.at[p, 1], g3_r.at[p, 1])
         for half in range(2):
             rows = srx[p][half].reshape(256, CW[p])
             if p:
@@ -402,7 +384,7 @@
         for dq in STEPS:
             send(
                 utx[p].at[half, coordinate(p, 2, dq), a2], spot,
-                q3_s.at[p, rel, dq, half], q3_r.at[p, rel, dq, c], near(p, 2, dq, half),
+                q3_s.at[p, 0], q3_r.at[p, rel, 0], near(p, 2, dq, half),
             )
 
     for half in range(2):
@@ -417,41 +399,36 @@
             if rel != 2:
                 for half in range(2):
                     give_back(p, half, rel)
-            send(utx[p].at[1 - c, a3, a2], urx[p].at[a2, a3, c], q3_s.at[p, rel, 0, 0], q3_r.at[p, rel, 0, 0], sib)
+            send(utx[p].at[1 - c, a3, a2], urx[p].at[a2, a3, c], q3_s.at[p, 1], q3_r.at[p, rel, 1], sib)
             urx[p][a2, a3, c] = utx[p][c, a3, a2]
 
     for rel in (2, 1, 3, 0):
         for p in range(3):
             a2 = coordinate(p, 1, rel)
-            for dq in STEPS:
-                for core in range(2):
-                    arrived(
-                        urx[p].at[a2, coordinate(p, 2, 4 - dq), core],
-                        q3_s.at[p, rel, dq, core], q3_r.at[p, rel, dq, core],
-                    )
-            arrived(urx[p].at[a2, coordinate(p, 2, 0), 1 - c], q3_s.at[p, rel, 0, 0], q3_r.at[p, rel, 0, 0])
+            arrived(urx[p].at[a2, few], q3_s.at[p, 0], q3_r.at[p, rel, 0])
+            arrived(urx[p].at[a2, 0, 0], q3_s.at[p, 1], q3_r.at[p, rel, 1])
             sums = lax.dot_general(
                 sel[p, rel], urx[p][a2].reshape(128, CW[p]), (((0,), (0,)), ((), ())), preferred_element_type=F32
             )
             if rel:
                 ltx[p][rel - 1] = sums.astype(BF16).reshape(4, 16, CW[p])
-                send(ltx[p].at[rel - 1], lrx[p].at[rel - 1], q2_s.at[p, rel - 1], q2_r.at[p, rel - 1], near(p, 1, rel))
+                send(ltx[p].at[rel - 1], lrx[p].at[rel - 1], q2_s.at[p], q2_r.at[p], near(p, 1, rel))
             else:
                 line[p][...] = sums.reshape(4, 16, CW[p])
     for p in range(3):
         total = line[p][...]
-        for k in (1, 0, 2):
-            arrived(lrx[p].at[k], q2_s.at[p, k], q2_r.at[p, k])
+        arrived(lrx[p], q2_s.at[p], q2_r.at[p])
+        for k in range(3):
             total = total + lrx[p][k].astype(F32)
         line[p][...] = total
         btx[p][...] = total.astype(BF16)
         for k, d in enumerate(STEPS):
-            send(btx[p].at[coordinate(p, 0, d)], brx[p].at[k], q1_s.at[p, k], q1_r.at[p, k], near(p, 0, d))
+            send(btx[p].at[coordinate(p, 0, d)], brx[p].at[k], q1_s.at[p], q1_r.at[p], near(p, 0, d))
     pieces = []
     for p in range(3):
         total = line[p][coordinate(p, 0, 0)]
+        arrived(brx[p], q1_s.at[p], q1_r.at[p])
         for k in range(3):
-            arrived(brx[p].at[k], q1_s.at[p, k], q1_r.at[p, k])
             total = total + brx[p][k].astype(F32)
         pieces.append(total)
     mixed = (kept[...] + jnp.concatenate(pieces, axis=1)).astype(BF16).astype(F32)
@@ -461,8 +438,23 @@
     arrived(fin_rx, pair_s.at[4], pair_r.at[4])
     out[:, other_cols] = fin_rx[...].astype(BF16)
 
-    for copy in sends:
-        copy.wait_send()
+    for i, view in ((0, res_tx), (2, sq_tx), (3, table.at[:, :, :, c]), (4, fin_tx)):
+        sent(view, pair_s.at[i])
+    sent(att.at[pl.ds(1, 7)], a2a_s.at[0])
+    sent(att_rx.at[:, c], af_s.at[0])
+    sent(y_tx.at[pl.ds(1, 7)], y_s.at[0])
+    sent(table.at[few, y, z, c], sh_s.at[0])
+    sent(table.at[:, few, z, c], sh_s.at[1])
+    sent(table.at[:, :, few, c], sh_s.at[2])
+    for p in range(3):
+        sent(at(p, few, 0), g1_s.at[p])
+        sent(at(p, few, slice(None)), g2_s.at[p])
+        sent(stx[p].at[:, few], g3_s.at[p, 0])
+        sent(stx[p].at[:, 0, 0], g3_s.at[p, 1])
+        sent(utx[p].at[:, few], q3_s.at[p, 0])
+        sent(utx[p].at[0, 0], q3_s.at[p, 1])
+        sent(ltx[p], q2_s.at[p])
+        sent(btx[p].at[few], q1_s.at[p])
 
 
 def local(
@@ -496,10 +488,9 @@
         *[v(4, 16, w) for w in CW],
         *[v(3, 16, w) for w in CW],
         v(16, HALF, dtype=F32), v(8, HALF, dtype=F32), v(8, HALF, dtype=F32),
-        dma((7,)), dma((8,)), dma((5,)), dma((5,)), dma((8,)), dma((8,)), dma((8,)), dma((8,)), dma((4, 8)), dma((4, 8)),
-        dma((3, 3)), dma((3, 3)), dma((3, 3)), dma((3, 3)), dma((3, 4, 3)), dma((3, 4, 3)),
-        dma((3, 4, 4, 2)), dma((3, 4, 4, 2)), dma((3, 4, 4, 2)), dma((3, 4, 4, 2)),
-        dma((3, 3)), dma((3, 3)), dma((3, 3)), dma((3, 3)),
+        dma((7,)), dma((8,)), dma((5,)), dma((5,)), dma((1,)), dma((8,)), dma((1,)), dma((1,)), dma((1,)), dma((1,)),
+        dma((3,)), dma((3,)), dma((3,)), dma((3, 3)), dma((3,)), dma((3, 3)),
+        dma((3, 2)), dma((3, 2)), dma((3, 2)), dma((3, 4, 2)), dma((3,)), dma((3,)), dma((3,)), dma((3,)),
     ]
     return pl.pallas_call(
         kernel,

time: 75.4 us -> 70.1 us (0.930)
  Pallas kernels: 73.7 us -> 68.5 us
    pallas_call x1, Pallas kernels: 73.7 us -> 68.5 us  [local(): pl.pallas_call(kernel, out_shape=jax.ShapeDtypeStruct((ROWS, D), BF16), i...]
where the time goes in v3:
time: 70.1 us; the launch traced here: 70 us
  Pallas kernels  68.5 us (98%)
  local copies, waits for them, and re-layouts  1.47 us (2%)
    pallas_call x1, Pallas kernels, local(): pl.pallas_call(kernel, out_shape=jax.ShapeDtypeStruct((ROWS, D), BF16), i...  68.5 us
    unnamed x1, local copies, waits for them, and re-layouts  1.47 us

profile of v3, /device:TPU:1, one launch (start us, length us, event | category | flops | bytes accessed | tf_op | source)
XLA Modules:
  0.0 70.0 jit_solution(4473495484013845598)
XLA Ops:
  0.0 68.5 %shard_map.136 = bf16[8,4096]{1,0:T(8,128)(2,1)} custom-call(bf16[8,4096]{1,0:T(8,128)(2,1)} %residual_in.1, bf16[8,8192]{1,0:T(8,128)(2,1)} %queries_in.1, bf16[8,256,512]{2,1,0:T(8,128)(2,1)} %key_cache.1, bf16[8,256,512]{2,1,0:T(8,128)(2,1)} %value_cache.1, bf16[8,512]{1,0:T(8,128)(2,1)} %new_keys_in.1, bf16[8,512]{1,0:T(8,128)(2,1)} %new_values_in.1, ...), custom_call_target="tpu_custom_call" | custom-call | flops 12000000000 | bytes 25165824 | tf_op jit(solution)/shard_map/pallas_call | solution.py:495
  68.5 1.5 %copy.16 = bf16[8,4096]{1,0:T(8,128)(2,1)} copy(bf16[8,4096]{1,0:T(8,128)(2,1)} %shard_map.136) | data formatting | bytes 131072

commit v4 on v3

--- a/solution.py
+++ b/solution.py
@@ -137,6 +137,14 @@
     for r in range(ROWS):
         limit = jnp.where(row_request == r, lengths[r], limit)
     visible = lax.broadcasted_iota(jnp.int32, (128, CACHE), 1) < limit
+    def send_heads(n):
+        same_side = lax.div(x, 2) == n // 4
+        target = device((jnp.where(same_side, x, 3 - x), n % 4, z), c)
+
+        @pl.when(n_me != n)
+        def _():
+            send(att.at[n], att_rx.at[n_me, c], a2a_s.at[0], a2a_r.at[n_me], target)
+
     for g in range(KVH):
         cols = slice(g * HD, (g + 1) * HD)
         q = jnp.concatenate(
@@ -164,14 +172,15 @@
         got = jnp.dot(spread, values[:, :, cols].reshape(ROWS * CACHE, HD), preferred_element_type=F32)
         got = got + own * jnp.concatenate([new_values[:, cols].astype(F32)] * 16, axis=0)
         att[2 * g : 2 * g + 2] = got.astype(BF16).reshape(2, 64, HD)
-
-    pl.semaphore_wait(barrier, len(partners))
+        if g == 2:
+            pl.semaphore_wait(barrier, len(partners))
+            for n in range(6):
+                send_heads(n)
+    for n in (6, 7):
+        send_heads(n)
+
     mine = pltpu.make_async_copy(att.at[n_me], att_rx.at[n_me, c], lsem.at[6])
     mine.start()
-    for i, (dx, dy) in enumerate(group):
-        if i:
-            target, n = member(dx, dy)
-            send(att.at[n], att_rx.at[n_me, c], a2a_s.at[0], a2a_r.at[i], device(target, c))
     for copy in arguments[4:]:
         copy.wait()
     probs = gate_probs[...]
@@ -206,7 +215,7 @@
         _, n = member(dx, (4 - dy) % 4)
         view = att_rx.at[n, c]
         if i:
-            arrived(view, a2a_s.at[0], a2a_r.at[i])
+            arrived(view, a2a_s.at[0], a2a_r.at[n])
         send(view, view, af_s.at[0], af_r.at[0], sib)
     arrived(att_rx.at[:, 1 - c], af_s.at[0], af_r.at[0])
 

time: 70.1 us -> 69 us (0.984)
  Pallas kernels: 68.5 us -> 67.3 us
    pallas_call x1, Pallas kernels: 68.5 us -> 67.3 us  [local(): pl.pallas_call(kernel, out_shape=jax.ShapeDtypeStruct((ROWS, D), BF16), i...]
where the time goes in v4:
time: 69 us; the launch traced here: 68.8 us
  Pallas kernels  67.3 us (98%)
  local copies, waits for them, and re-layouts  1.47 us (2%)
    pallas_call x1, Pallas kernels, local(): pl.pallas_call(kernel, out_shape=jax.ShapeDtypeStruct((ROWS, D), BF16), i...  67.3 us
    unnamed x1, local copies, waits for them, and re-layouts  1.47 us

profile of v4, /device:TPU:1, one launch (start us, length us, event | category | flops | bytes accessed | tf_op | source)
XLA Modules:
  0.0 68.8 jit_solution(566557968599226487)
XLA Ops:
  0.0 67.3 %shard_map.136 = bf16[8,4096]{1,0:T(8,128)(2,1)} custom-call(bf16[8,4096]{1,0:T(8,128)(2,1)} %residual_in.1, bf16[8,8192]{1,0:T(8,128)(2,1)} %queries_in.1, bf16[8,256,512]{2,1,0:T(8,128)(2,1)} %key_cache.1, bf16[8,256,512]{2,1,0:T(8,128)(2,1)} %value_cache.1, bf16[8,512]{1,0:T(8,128)(2,1)} %new_keys_in.1, bf16[8,512]{1,0:T(8,128)(2,1)} %new_values_in.1, ...), custom_call_target="tpu_custom_call" | custom-call | flops 12000000000 | bytes 25165824 | tf_op jit(solution)/shard_map/pallas_call | solution.py:504
  67.3 1.5 %copy.16 = bf16[8,4096]{1,0:T(8,128)(2,1)} copy(bf16[8,4096]{1,0:T(8,128)(2,1)} %shard_map.136) | data formatting | bytes 131072
